TPU v7x, 128 devices: a whole 4x4x4 slice. The times are simulated.
128 devices in a mesh: gx: 16 (over y_hi, x, core), gy: 8 (over z, y_lo).
Axes of the slice: x: 4, y: 4 (y_hi: 2, y_lo: 2; y = y_hi * 2 + y_lo), z: 4, core: 2. Of those that a mesh axis runs over, the one named last changes fastest.
Arguments:
- tendencies: bfloat16 [8192, 2, 24, 16, 128], P(('gx', 'gy')), may hold values from -6 to 6
- thickness: float32 [24], replicated, may hold values from 0.1 to 0.4
- ocean_blocks: int32 [8192], replicated, may hold values from 0 to 10239, as said below
- land_mask: int32 [2560, 8192], P('gy', 'gx'), may hold values from 0 to 1, as said below
- implicit_term: float32 [2560, 8192], P('gy', 'gx'), may hold values from 0.05 to 0.5
- first_guess: float32 [2560, 8192], P('gy', 'gx'), may hold values from -6 to 6
Outputs:
- solution: float32 [2560, 8192], P('gy', 'gx')
- residual: float32 [2560, 8192], P('gy', 'gx')
- gradient_blocks: float32 [8192, 2, 16, 128], P(('gx', 'gy'))
Inputs may be any that keep to these rules, and one draw needn't show every extreme that they name: `ocean_blocks`: distinct global indices p * 64 + q of ocean blocks (block row p, block column q). Every device's tile holds exactly 64 listed blocks, and the 64 entries that one device holds lie in the tiles of exactly 64 devices, 1 in each. `land_mask`: every cell of a block that ocean_blocks does not list is 0.
All inputs are finite; a program needn't handle non-finite values.
Results may differ from a plain program's by a relative error of at most 0.0003.
Values sent between devices are 32-bit elements; how exact they have to be, the bound alone decides.
No kernel may reach another device: no remote copies, remote signals or barrier semaphores. Data moves between devices by JAX's collectives and lax.ppermute only.
A program may use at most 128 MiB of HBM per device.

v0:
```python
import functools

import jax
import jax.numpy as jnp
from jax import lax
from jax.experimental import pallas as pl
from jax.experimental.pallas import tpu as pltpu
from jax.sharding import PartitionSpec as P

BX = 128
BY = 16
BCOL = 4
BROW = 20
LEV = 24
ITERS = 4
STENCIL_SUM = 5.0
CORNER_WEIGHT = 0.25
LOWER_BOUND = 0.02
UPPER_BOUND = 2.0

F32 = jnp.float32
OWN = BROW + 4
EXT = 32
OFF = 8
DEPTH = 4
WIDE = BCOL * BX + BX
STRIP = DEPTH * BY + 8
BATCH = 8
VMEM_LIMIT = 48 << 20


def call(kernel, out_shape, operands, scratch=(), cost=1.0):
    spaces = [
        pl.BlockSpec(memory_space=pltpu.SMEM if a.dtype == jnp.int32 and a.ndim == 1 else pltpu.VMEM)
        for a in operands
    ]
    size = sum(a.size * a.dtype.itemsize for a in operands)
    return pl.pallas_call(
        kernel,
        out_shape=[jax.ShapeDtypeStruct(s, F32) for s in out_shape],
        in_specs=spaces,
        out_specs=[pl.BlockSpec(memory_space=pltpu.VMEM) for _ in out_shape],
        scratch_shapes=[pltpu.VMEM(s, F32) for s in scratch],
        compiler_params=pltpu.CompilerParams(vmem_limit_bytes=VMEM_LIMIT),
        cost_estimate=pl.CostEstimate(
            flops=int(cost * 4e6), bytes_accessed=int(size), transcendentals=0
        ),
    )(*operands)


def lanes(shape):
    return lax.broadcasted_iota(jnp.int32, shape, 1)


def rows(shape):
    return lax.broadcasted_iota(jnp.int32, shape, 0)


def pack(tiles, last):
    lane = lanes(tiles[0].shape)
    packed = jnp.zeros(tiles[0].shape, F32)
    for p, tile in enumerate(tiles):
        shift = (8 * p + 8 if last else 8 * p) % BX
        moved = pltpu.roll(tile, shift, 1) if shift else tile
        packed = jnp.where(lane // 8 == p, moved, packed)
    return packed


def unpack(packed, p, at):
    shift = (at - 8 * p) % BX
    return pltpu.roll(packed, shift, 1) if shift else packed


def side_tile(east, west, p):
    lane = lanes(east.shape)
    tile = jnp.where(lane < 8, unpack(east, p, 0), 0.0)
    return jnp.where(lane >= BX - 8, unpack(west, p, BX - 8), tile)


def turned(strip):
    lane = BX - 1 - lanes((strip.shape[0], BX))
    tiles = [strip[:, BX * q : BX * q + BX] for q in range(WIDE // BX)]
    tiles = [jnp.take_along_axis(tile, lane, axis=1) for tile in tiles]
    return jnp.concatenate([tiles[(BCOL - 1 - q) % (BCOL + 1)] for q in range(BCOL + 1)], axis=1)


def write_strips(flags, field, top_extra, bottom_extra, first, second, top, bottom, flipped):
    odd = flags[0] == 1
    for p in range(BY):
        top[DEPTH * p : DEPTH * p + DEPTH, :] = field[p, BROW - DEPTH : BROW, :]
        bottom[DEPTH * p : DEPTH * p + DEPTH, :] = field[p, 0:DEPTH, :]
    tail = DEPTH * BY
    first_row = rows((8, WIDE)) == 0
    top[tail:STRIP, :] = jnp.where(first_row, top_extra, 0.0)
    bottom[tail:STRIP, :] = jnp.where(first_row, bottom_extra, 0.0)
    first[...] = jnp.where(odd, bottom[...], top[...])

    @pl.when(flags[1] == 1)
    def _():
        for r in range(tail):
            flipped[r : r + 1, :] = top[tail - 1 - r : tail - r, :]
        flipped[tail:STRIP, :] = top[tail:STRIP, :]
        second[...] = turned(flipped[...])

    @pl.when(flags[1] == 0)
    def _():
        second[...] = jnp.where(odd, top[...], bottom[...])


def sums_kernel(dst, thickness, tendencies, out):
    step = pl.program_id(0)

    def block(n, carry):
        slot = dst[step * BATCH + n]
        for part in range(2):
            total = thickness[0] * tendencies[n, part, 0].astype(F32)
            for level in range(1, LEV):
                total = total + thickness[level] * tendencies[n, part, level].astype(F32)
            out[slot, part] = total
        return carry

    lax.fori_loop(0, BATCH, block, 0)


def prepare_kernel(mask, implicit, guess, diag, start, to_east, to_west, work):
    for q in range(BCOL):
        cols = slice(BX * q, BX * q + BX)
        m = mask[:, cols].astype(F32)
        work[q] = m * (STENCIL_SUM + implicit[:, cols]) + (1.0 - m)
        work[BCOL + q] = m * guess[:, cols]
    for k, field in enumerate((diag, start)):
        first, last = [], []
        for p in range(BY):
            for q in range(BCOL):
                tile = work[BCOL * k + q, pl.ds(p, BROW, stride=BY), :]
                tile = jnp.concatenate([tile, jnp.zeros((OWN - BROW, BX), F32)], axis=0)
                field[p, :, BX * q : BX * q + BX] = tile
                if q == 0:
                    first.append(tile)
                if q == BCOL - 1:
                    last.append(tile)
        to_east[OWN * k : OWN * k + OWN, :] = pack(last, True)
        to_west[OWN * k : OWN * k + OWN, :] = pack(first, False)


def widen_kernel(flags, diag, start, east, west, diag_wide, start_wide, first, second, *work):
    for k, (field, wide) in enumerate(((diag, diag_wide), (start, start_wide))):
        part = slice(OWN * k, OWN * k + OWN)
        for p in range(BY):
            wide[p, :, 0 : BCOL * BX] = field[p]
            wide[p, :, BCOL * BX : WIDE] = side_tile(east[part, :], west[part, :], p)
    write_strips(
        flags,
        diag_wide,
        start_wide[BY - 1, BROW - 1 : BROW, :],
        start_wide[0, 0:1, :],
        first,
        second,
        *work,
    )


def assemble(flags, field, first, second, out):
    odd = flags[0] == 1
    for p in range(BY):
        part = slice(DEPTH * p, DEPTH * p + DEPTH)
        out[p, 0 : OFF - DEPTH, :] = jnp.zeros((OFF - DEPTH, WIDE), F32)
        out[p, OFF - DEPTH : OFF, :] = jnp.where(odd, first[part, :], second[part, :])
        out[p, OFF : OFF + BROW, :] = field[p, 0:BROW, :]
        out[p, OFF + BROW : EXT, :] = jnp.where(odd, second[part, :], first[part, :])
    tail = DEPTH * BY
    north = jnp.where(odd, second[tail : tail + 1, :], first[tail : tail + 1, :])
    south = jnp.where(odd, first[tail : tail + 1, :], second[tail : tail + 1, :])
    return north, south


def beside(value):
    return pltpu.roll(value, 1, 1) + pltpu.roll(value, WIDE - 1, 1)


def factor_kernel(flags, diag, start, first, second, diag_full, inverse, start_full, minus_a, tall):
    north, south = assemble(flags, diag, first, second, diag_full)
    previous = jnp.zeros((EXT, WIDE), F32)
    for p in range(BY):
        d = diag_full[p]
        previous = jnp.where(d > 1.0, 1.0 / (d - previous), 0.0)
        inverse[p] = previous
    row = rows((EXT, WIDE))
    for p in range(BY):
        start_full[p, 0:OFF, :] = jnp.zeros((OFF, WIDE), F32)
        start_full[p, OFF:EXT, :] = start[p]
    start_full[0] = jnp.where(row == OFF + BROW, north, start_full[0])
    below = jnp.where(row == OFF - 1, south, start_full[BY - 1])
    for p in range(BY):
        x = start_full[p]
        tall[p] = x + CORNER_WEIGHT * beside(x)
    below = pltpu.roll(below + CORNER_WEIGHT * beside(below), 1, 0)
    for p in range(BY):
        x = start_full[p]
        south_part = tall[p - 1] if p > 0 else below
        north_part = tall[p + 1] if p + 1 < BY else pltpu.roll(tall[0], EXT - 1, 0)
        value = beside(x) + south_part + north_part - diag_full[p] * x
        minus_a[p] = value[OFF:EXT, 0 : BCOL * BX]


def place_kernel(loc, arrived, diag, minus_a, right, f1_top, to_east, to_west, work):
    def put(slot, carry):
        index = loc[slot]
        row, col = index >> 2, index & 3
        work[col, pl.ds(row, BY, stride=OWN), :] = arrived[slot, 0]
        work[BCOL + col, pl.ds(row, BY, stride=OWN), :] = arrived[slot, 1]
        return carry

    lax.fori_loop(0, arrived.shape[0], put, 0, unroll=8)
    lane = lanes((OWN, BX))
    row = rows((OWN, BX))
    first, last = [], []
    for q in range(BCOL):
        cols = slice(BX * q, BX * q + BX)

        def part(component, p, at):
            value = work[BCOL * component + at, OWN * p : OWN * p + OWN, :]
            return jnp.where(diag[p, :, BX * at : BX * at + BX] > 1.0, value, 0.0)

        south = jnp.where(row == 0, 0.0, pltpu.roll(part(1, BY - 1, q), 1, 0))
        for p in range(BY):
            f0 = part(0, p, q)
            f1 = part(1, p, q)
            west = pltpu.roll(f0, 1, 1)
            edge = pltpu.roll(part(0, p, q - 1), 1, 1) if q else 0.0
            west = jnp.where(lane == 0, edge, west)
            value = (f0 - west) + (f1 - south) + minus_a[p, :, cols]
            right[p, :, cols] = value
            south = f1
            if q == 0:
                first.append(value)
            if q == BCOL - 1:
                last.append(jnp.where(lane == BX - 5, pltpu.roll(f0, BX - 4, 1), value))
        f1_top[:, cols] = jnp.broadcast_to(south[BROW - 1 : BROW, :], (8, BX))
    to_west[...] = jnp.where(row == BROW, f1_top[0:1, 0:BX], pack(first, False))
    to_east[...] = jnp.where(row == BROW, f1_top[0:1, BX * (BCOL - 1) : BX * BCOL], pack(last, True))


def widen_right_kernel(flags, right, f1_top, mine, east, west, wide, f1_wide, first, second, *work):
    lane = lanes((OWN, BX))
    for p in range(BY):
        wide[p, :, BX : BCOL * BX] = right[p, :, BX:]
        wide[p, :, 0:BX] = right[p, :, 0:BX] - jnp.where(lane == 0, unpack(west[...], p, BX - 3), 0.0)
        tile = side_tile(east[...], west[...], p)
        wide[p, :, BCOL * BX : WIDE] = tile - jnp.where(lane == 0, unpack(mine[...], p, BX - 3), 0.0)
    f1_wide[:, 0 : BCOL * BX] = f1_top[...]
    lane = lanes((8, BX))
    tile = jnp.where(lane < 8, east[BROW : BROW + 1, :], 0.0)
    tile = jnp.where(lane >= BX - 8, west[BROW : BROW + 1, :], tile)
    f1_wide[:, BCOL * BX : WIDE] = tile
    write_strips(
        flags, wide, f1_wide[0:1, :], jnp.zeros((1, WIDE), F32), first, second, *work
    )


def solve_kernel(
    flags, loc, right, f1_wide, first, second, diag, inverse, start,
    solution, residual, slots,
    r_all, f_all, t_all, u_all, g_all, natural,
):
    north, south = assemble(flags, right, first, second, r_all)
    row = rows((EXT, WIDE))
    fold = jnp.where(flags[1] == 1, 0.0, 1.0)
    fix = jnp.where(row == OFF, south, 0.0)
    fix = fix + jnp.where(row == OFF + BROW, fold * f1_wide[0:1, :], 0.0)
    r_all[0] = r_all[0] - fix

    def gathered(p):
        below = t_all[p - 1] if p > 0 else pltpu.roll(t_all[BY - 1], 1, 0)
        above = t_all[p + 1] if p + 1 < BY else pltpu.roll(t_all[0], EXT - 1, 0)
        return r_all[p] + (below + above)

    gamma = (UPPER_BOUND + LOWER_BOUND) / 2.0
    alpha = 2.0 / (UPPER_BOUND - LOWER_BOUND)
    scale = 4.0 * alpha * alpha
    omega = 2.0 / gamma
    for k in range(ITERS):
        if k > 0:
            omega = 1.0 / (gamma - omega / scale)
        f = None
        for p in range(BY):
            if k > 0:
                r = gathered(p)
                r_all[p] = r
            else:
                r = r_all[p]
            f = (r if f is None else r + f) * inverse[p]
            f_all[p] = f
        s = None
        for p in reversed(range(BY)):
            s = f_all[p] if s is None else f_all[p] + inverse[p] * s
            if k == 0:
                u = s * (1.0 / gamma)
            else:
                u = omega * s + (gamma * omega - 1.0) * u_all[k - 1, p]
            u_all[k, p] = u
            h = beside(u)
            t_all[p] = u + CORNER_WEIGHT * h
            r_all[p] = r_all[p] + (h - diag[p] * u)
    for p in range(BY):
        r = jnp.where(diag[p] > 1.0, gathered(p), 0.0)
        x = start[p] + ((u_all[0, p] + u_all[1, p]) + (u_all[2, p] + u_all[3, p]))
        f_all[p] = x
        for q in range(BCOL):
            cols = slice(BX * q, BX * q + BX)
            natural[q, pl.ds(p, BROW, stride=BY), :] = x[OFF : OFF + BROW, cols]
            natural[BCOL + q, pl.ds(p, BROW, stride=BY), :] = r[OFF : OFF + BROW, cols]
    for q in range(BCOL):
        cols = slice(BX * q, BX * q + BX)
        solution[:, cols] = natural[q]
        residual[:, cols] = natural[BCOL + q]
    for p in range(BY):
        x = f_all[p]
        ocean = diag[p] > 1.0
        above = f_all[p + 1] if p + 1 < BY else pltpu.roll(f_all[0], EXT - 1, 0)
        zonal = jnp.where(ocean, pltpu.roll(x, WIDE - 1, 1) - x, 0.0)
        meridional = jnp.where(ocean, above - x, 0.0)
        for q in range(BCOL):
            cols = slice(BX * q, BX * q + BX)
            g_all[q, EXT * p : EXT * p + EXT, :] = zonal[:, cols]
            g_all[BCOL + q, EXT * p : EXT * p + EXT, :] = meridional[:, cols]

    def take(slot, carry):
        index = loc[slot]
        row, col = (index >> 2) + OFF, index & 3
        slots[slot, 0] = g_all[col, pl.ds(row, BY, stride=EXT), :]
        slots[slot, 1] = g_all[BCOL + col, pl.ds(row, BY, stride=EXT), :]
        return carry

    lax.fori_loop(0, slots.shape[0], take, 0, unroll=8)


def pick_kernel(dst, slots, out, sems):
    copies = [
        pltpu.make_async_copy(slots.at[dst[n]], out.at[n], sems.at[n]) for n in range(out.shape[0])
    ]
    for copy in copies:
        copy.start()
    for copy in copies:
        copy.wait()


def body(tendencies, thickness, ocean_blocks, land_mask, implicit_term, first_guess):
    nx = lax.axis_size("gx")
    ny = lax.axis_size("gy")
    gx = lax.axis_index("gx")
    gy = lax.axis_index("gy")
    devices = nx * ny
    listed = tendencies.shape[0]
    me = gx * ny + gy
    block_cols = BCOL * nx
    block_row = ocean_blocks // block_cols
    block_col = ocean_blocks % block_cols
    owner = block_col // BCOL * ny + block_row // BROW
    local = block_row % BROW * BCOL + block_col % BCOL
    dst = lax.dynamic_slice_in_dim(owner, me * listed, listed)
    loc = jnp.min(jnp.where(owner == me, local, BROW * BCOL).reshape(devices, listed), axis=1)
    flags = jnp.stack([gy % 2, (gy == ny - 1).astype(jnp.int32)]).astype(jnp.int32)

    east = [(i, (i + 1) % nx) for i in range(nx)]
    west = [(j, i) for i, j in east]
    swap_a, swap_b = [], []
    for i in range(nx):
        for j in range(ny):
            swap_a.append((i * ny + j, i * ny + (j ^ 1)))
            if j == ny - 1:
                swap_b.append((i * ny + j, (nx - 1 - i) * ny + j))
            elif j > 0:
                swap_b.append((i * ny + j, i * ny + (j + 1 if j % 2 else j - 1)))

    def exchange_x(to_east, to_west):
        return lax.ppermute(to_west, "gx", west), lax.ppermute(to_east, "gx", east)

    def exchange_y(first, second):
        return lax.ppermute(first, ("gx", "gy"), swap_a), lax.ppermute(second, ("gx", "gy"), swap_b)

    sums = pl.pallas_call(
        sums_kernel,
        grid_spec=pltpu.PrefetchScalarGridSpec(
            num_scalar_prefetch=2,
            grid=(listed // BATCH,),
            in_specs=[pl.BlockSpec((BATCH, 2, LEV, BY, BX), lambda i, *_: (i, 0, 0, 0, 0))],
            out_specs=pl.BlockSpec((devices, 2, BY, BX), lambda i, *_: (0, 0, 0, 0)),
        ),
        out_shape=jax.ShapeDtypeStruct((devices, 2, BY, BX), F32),
        compiler_params=pltpu.CompilerParams(vmem_limit_bytes=VMEM_LIMIT),
    )(dst, thickness, tendencies)
    arrived = lax.all_to_all(sums, ("gx", "gy"), split_axis=0, concat_axis=0, tiled=True)

    own = (BY, OWN, BCOL * BX)
    wide = (BY, OWN, WIDE)
    full = (BY, EXT, WIDE)
    strip = (STRIP, WIDE)
    diag, start, to_east, to_west = call(
        prepare_kernel,
        [own, own, (2 * OWN, BX), (2 * OWN, BX)],
        [land_mask, implicit_term, first_guess],
        [(2 * BCOL, BROW * BY, BX)],
    )
    diag, start, first, second = call(
        widen_kernel,
        [wide, wide, strip, strip],
        [flags, diag, start, *exchange_x(to_east, to_west)],
        [strip, strip, strip],
    )
    diag_full, inverse, start_full, minus_a = call(
        factor_kernel,
        [full, full, full, own],
        [flags, diag, start, *exchange_y(first, second)],
        [full],
    )
    right, f1_top, to_east, to_west = call(
        place_kernel,
        [own, (8, BCOL * BX), (OWN, BX), (OWN, BX)],
        [loc, arrived, diag, minus_a],
        [(2 * BCOL, BY * OWN, BX)],
    )
    right, f1_wide, first, second = call(
        widen_right_kernel,
        [wide, (8, WIDE), strip, strip],
        [flags, right, f1_top, to_east, *exchange_x(to_east, to_west)],
        [strip, strip, strip],
    )
    solution, residual, slots = call(
        solve_kernel,
        [(BROW * BY, BCOL * BX), (BROW * BY, BCOL * BX), (devices, 2, BY, BX)],
        [flags, loc, right, f1_wide, *exchange_y(first, second), diag_full, inverse, start_full],
        [
            full,
            full,
            full,
            (ITERS, *full),
            (2 * BCOL, BY * EXT, BX),
            (2 * BCOL, BROW * BY, BX),
        ],
        4.0,
    )
    returned = lax.all_to_all(slots, ("gx", "gy"), split_axis=0, concat_axis=0, tiled=True)
    gradient_blocks = pl.pallas_call(
        pick_kernel,
        out_shape=jax.ShapeDtypeStruct((listed, 2, BY, BX), F32),
        in_specs=[pl.BlockSpec(memory_space=pltpu.SMEM), pl.BlockSpec(memory_space=pl.ANY)],
        out_specs=pl.BlockSpec(memory_space=pl.ANY),
        scratch_shapes=[pltpu.SemaphoreType.DMA((listed,))],
    )(dst, returned)
    return solution, residual, gradient_blocks


def solution(mesh):
    placed = (
        P(("gx", "gy"), None, None, None, None),
        P(),
        P(),
        P("gy", "gx"),
        P("gy", "gx"),
        P("gy", "gx"),
    )
    return jax.shard_map(
        body,
        mesh=mesh,
        in_specs=placed,
        out_specs=(P("gy", "gx"), P("gy", "gx"), P(("gx", "gy"), None, None, None)),
        check_vma=False,
    )
```

profile of v0, /device:TPU:1, one launch (start us, length us, event | category | flops | bytes accessed | tf_op | source)
XLA Modules:
  0.0 178.1 jit_solution(13695014547637802167)
XLA Ops:
  2.2 8.7 %shard_map.85 = f32[128,2,16,128]{3,2,1,0:T(8,128)S(1)} custom-call(s32[64]{0:T(128)S(1)} %dynamic_slice.3.dst, f32[24]{0:T(128)S(1)} %copy-done.18, bf16[64,2,24,16,128]{4,3,2,1,0:T(8,128)(2,1)} %tendencies.1), custom_call_target="tpu_custom_call" | custom-call | tf_op jit(solution)/shard_map/pallas_call | solution.py:382
  11.0 1.3 copy-done
  12.3 11.5 %all-to-all-start = ((f32[128,2,16,128]{3,2,1,0:T(8,128)}), f32[128,2,16,128]{3,2,1,0:T(8,128)S(1)}, u32[]{:S(2)}, u32[]{:S(2)}) async-start(f32[128,2,16,128]{3,2,1,0:T(8,128)} %copy-done), calls=%async_computation | async-start | bytes 4194304 | tf_op jit(solution)/shard_map/all_to_all | solution.py:393
  23.9 1.1 copy-done.16
  27.4 1.1 collective-permute-start
  29.3 19.3 %collective-permute-done.east = f32[48,128]{1,0:T(8,128)S(1)} collective-permute-done((f32[48,128]{1,0:T(8,128)S(1)}, f32[48,128]{1,0:T(8,128)S(1)}, u32[]{:S(2)}, u32[]{:S(2)}) %collective-permute-start) | collective-permute-done | bytes 24608 | tf_op jit(solution)/shard_map/ppermute | solution.py:377
  48.6 1.1 copy-done.9
  49.7 1.1 copy-done.11
  50.8 1.6 shard_map.87
  52.4 0.9 copy-done.6
  53.4 1.2 collective-permute-start.2
  55.4 2.6 %collective-permute-done.2.first = f32[72,640]{1,0:T(8,128)S(1)} collective-permute-done((f32[72,640]{1,0:T(8,128)}, f32[72,640]{1,0:T(8,128)S(1)}, u32[]{:S(2)}, u32[]{:S(2)}) %collective-permute-start.2) | collective-permute-done | bytes 184352 | tf_op jit(solution)/shard_map/ppermute | solution.py:380
  58.0 1.2 copy-done.7
  59.2 2.8 %shard_map.88 = (f32[16,32,640]{2,1,0:T(8,128)S(1)}, f32[16,32,640]{2,1,0:T(8,128)S(1)}, f32[16,32,640]{2,1,0:T(8,128)}, f32[16,24,512]{2,1,0:T(8,128)S(1)}) custom-call(s32[2]{0:T(128)S(1)} %pad_add_fusion.flags, f32[16,24,640]{2,1,0:T(8,128)S(1)} %get-tuple-element.30.diag, f32[16,24,640]{2,1,0:T(8,128)S(1)} %copy-done.7, ...), custom_call_target="tpu_custom_call" | custom-call | flops 4000000 | bytes 2334728 | tf_op jit(solution)/shard_map/pallas_call | solution.py:38
  62.0 1.1 copy-done.1
  63.1 1.1 copy-done.3
  65.1 1.1 copy-done.13
  66.2 1.6 shard_map.89
  67.8 6.9 %collective-permute-start.4 = (f32[24,128]{1,0:T(8,128)S(1)}, f32[24,128]{1,0:T(8,128)S(1)}, u32[]{:S(2)}, u32[]{:S(2)}) collective-permute-start(f32[24,128]{1,0:T(8,128)S(1)} %get-tuple-element.38), channel_id=1, source_target_pairs={{8,0},{16,8},{24,16},{32,24},{40,32},{48,40},{56,48},{64,56},{72,6... | collective-permute-start | bytes 36872 | tf_op jit(solution)/shard_map/ppermute | solution.py:377
  76.8 3.6 %collective-permute-start.6 = (f32[72,640]{1,0:T(8,128)S(1)}, f32[72,640]{1,0:T(8,128)S(1)}, u32[]{:S(2)}, u32[]{:S(2)}) collective-permute-start(f32[72,640]{1,0:T(8,128)S(1)} %get-tuple-element.41), channel_id=1, source_target_pairs={{0,1},{1,0},{2,3},{3,2},{4,5},{5,4},{6,7},{7,6},{8,9},{9,8},{10,11... | collective-permute-start | bytes 552968 | tf_op jit(solution)/shard_map/ppermute | solution.py:380
  81.3 2.1 %collective-permute-done.6.first = f32[72,640]{1,0:T(8,128)S(1)} collective-permute-done((f32[72,640]{1,0:T(8,128)S(1)}, f32[72,640]{1,0:T(8,128)S(1)}, u32[]{:S(2)}, u32[]{:S(2)}) %collective-permute-start.6) | collective-permute-done | bytes 184352 | tf_op jit(solution)/shard_map/ppermute | solution.py:380
  83.4 10.6 %shard_map.91 = (f32[320,512]{1,0:T(8,128)}, f32[320,512]{1,0:T(8,128)}, f32[128,2,16,128]{3,2,1,0:T(8,128)}) custom-call(s32[2]{0:T(128)S(1)} %pad_add_fusion.flags, s32[128]{0:T(128)S(1)} %reduce_min.9.loc, f32[16,24,640]{2,1,0:T(8,128)S(1)} %get-tuple-element.39.right, f32[8,640]{1,0:T(8,128)S(1)} %get-tuple-element.40.f1_wide, ...), custom_call_target="tpu_custom_call" | custom-call | flops 16000000 | bytes 5304840 | tf_op jit(solution)/shard_map/pallas_call | solution.py:38
  94.0 49.9 %all_to_all.10.slots = f32[128,2,16,128]{3,2,1,0:T(8,128)} all-to-all(f32[128,2,16,128]{3,2,1,0:T(8,128)} %get-tuple-element.48), channel_id=1, replica_groups=mesh['gx'=16,'gy'=8] {'gx','gy'}, dimensions={0} | all-to-all | bytes 4194304 | tf_op jit(solution)/shard_map/all_to_all | solution.py:443
  143.9 34.1 %shard_map.92 = f32[64,2,16,128]{3,2,1,0:T(8,128)} custom-call(s32[64]{0:T(128)} %copy-done.17, f32[128,2,16,128]{3,2,1,0:T(8,128)} %all_to_all.10.slots), custom_call_target="tpu_custom_call" | custom-call | tf_op jit(solution)/shard_map/pallas_call | solution.py:444
  (46 shorter events, 9.5 us)
Async XLA Ops:
  2.2 8.7 %copy-start.17 = (s32[64]{0:T(128)}, s32[64]{0:T(128)S(1)}, u32[]{:S(2)}) copy-start(s32[64]{0:T(128)S(1)} %dynamic_slice.3.dst) | copy-start | bytes 772
  11.0 1.4 copy-start
  12.3 11.5 %copy-start.14 = (s32[320,512]{1,0:T(8,128)S(1)}, s32[320,512]{1,0:T(8,128)}, u32[]{:S(2)}) copy-start(s32[320,512]{1,0:T(8,128)} %mask.1) | copy-start | bytes 1966084
  12.3 11.5 %copy-start.15 = (f32[320,512]{1,0:T(8,128)S(1)}, f32[320,512]{1,0:T(8,128)}, u32[]{:S(2)}) copy-start(f32[320,512]{1,0:T(8,128)} %implicit.1) | copy-start | bytes 1966084
  12.3 52.7 %all-to-all-start = ((f32[128,2,16,128]{3,2,1,0:T(8,128)}), f32[128,2,16,128]{3,2,1,0:T(8,128)S(1)}, u32[]{:S(2)}, u32[]{:S(2)}) async-start(f32[128,2,16,128]{3,2,1,0:T(8,128)} %copy-done), calls=%async_computation | async-start | bytes 4194304 | tf_op jit(solution)/shard_map/all_to_all | solution.py:393
  23.9 1.1 copy-start.16
  27.4 21.1 %collective-permute-start = (f32[48,128]{1,0:T(8,128)S(1)}, f32[48,128]{1,0:T(8,128)S(1)}, u32[]{:S(2)}, u32[]{:S(2)}) collective-permute-start(f32[48,128]{1,0:T(8,128)S(1)} %get-tuple-element.28), channel_id=1, source_target_pairs={{8,0},{16,8},{24,16},{32,24},{40,32},{48,40},{56,48},{64,56},{72,6... | collective-permute-start | bytes 73736 | tf_op jit(solution)/shard_map/ppermute | solution.py:377
  28.5 20.1 %collective-permute-start.1 = (f32[48,128]{1,0:T(8,128)S(1)}, f32[48,128]{1,0:T(8,128)S(1)}, u32[]{:S(2)}, u32[]{:S(2)}) collective-permute-start(f32[48,128]{1,0:T(8,128)S(1)} %get-tuple-element.29), channel_id=1, source_target_pairs={{0,8},{8,16},{16,24},{24,32},{32,40},{40,48},{48,56},{56,64},{64,7... | collective-permute-start | bytes 73736 | tf_op jit(solution)/shard_map/ppermute | solution.py:377
  48.6 1.1 copy-start.9
  49.7 1.1 copy-start.11
  52.4 0.9 copy-start.6
  53.4 4.6 %collective-permute-start.2 = (f32[72,640]{1,0:T(8,128)}, f32[72,640]{1,0:T(8,128)S(1)}, u32[]{:S(2)}, u32[]{:S(2)}) collective-permute-start(f32[72,640]{1,0:T(8,128)} %get-tuple-element.32), channel_id=1, source_target_pairs={{0,1},{1,0},{2,3},{3,2},{4,5},{5,4},{6,7},{7,6},{8,9},{9,8},{10,11... | collective-permute-start | bytes 552968 | tf_op jit(solution)/shard_map/ppermute | solution.py:380
  54.6 3.4 %collective-permute-start.3 = (f32[72,640]{1,0:T(8,128)}, f32[72,640]{1,0:T(8,128)S(1)}, u32[]{:S(2)}, u32[]{:S(2)}) collective-permute-start(f32[72,640]{1,0:T(8,128)} %get-tuple-element.33), channel_id=1, source_target_pairs={{1,2},{2,1},{3,4},{4,3},{5,6},{6,5},{7,127},{9,10},{10,9},{11,12},... | collective-permute-start | bytes 552968 | tf_op jit(solution)/shard_map/ppermute | solution.py:380
  58.0 1.2 copy-start.7
  62.0 1.1 copy-start.1
  63.1 1.1 copy-start.3
  65.1 1.1 copy-start.13
  66.2 17.2 %copy-start.2 = (f32[16,32,640]{2,1,0:T(8,128)S(1)}, f32[16,32,640]{2,1,0:T(8,128)}, u32[]{:S(2)}) copy-start(f32[16,32,640]{2,1,0:T(8,128)} %copy-done.1) | copy-start | bytes 3932164
  66.2 17.2 %copy-start.4 = (f32[16,32,640]{2,1,0:T(8,128)S(1)}, f32[16,32,640]{2,1,0:T(8,128)}, u32[]{:S(2)}) copy-start(f32[16,32,640]{2,1,0:T(8,128)} %copy-done.3) | copy-start | bytes 3932164
  66.2 17.2 %copy-start.5 = (f32[16,32,640]{2,1,0:T(8,128)S(1)}, f32[16,32,640]{2,1,0:T(8,128)}, u32[]{:S(2)}) copy-start(f32[16,32,640]{2,1,0:T(8,128)} %get-tuple-element.45.start) | copy-start | bytes 3932164
  67.8 7.7 %collective-permute-start.4 = (f32[24,128]{1,0:T(8,128)S(1)}, f32[24,128]{1,0:T(8,128)S(1)}, u32[]{:S(2)}, u32[]{:S(2)}) collective-permute-start(f32[24,128]{1,0:T(8,128)S(1)} %get-tuple-element.38), channel_id=1, source_target_pairs={{8,0},{16,8},{24,16},{32,24},{40,32},{48,40},{56,48},{64,56},{72,6... | collective-permute-start | bytes 36872 | tf_op jit(solution)/shard_map/ppermute | solution.py:377
  74.8 1.2 collective-permute-start.5
  76.8 6.5 %collective-permute-start.6 = (f32[72,640]{1,0:T(8,128)S(1)}, f32[72,640]{1,0:T(8,128)S(1)}, u32[]{:S(2)}, u32[]{:S(2)}) collective-permute-start(f32[72,640]{1,0:T(8,128)S(1)} %get-tuple-element.41), channel_id=1, source_target_pairs={{0,1},{1,0},{2,3},{3,2},{4,5},{5,4},{6,7},{7,6},{8,9},{9,8},{10,11... | collective-permute-start | bytes 552968 | tf_op jit(solution)/shard_map/ppermute | solution.py:380
  80.5 2.9 %collective-permute-start.7 = (f32[72,640]{1,0:T(8,128)S(1)}, f32[72,640]{1,0:T(8,128)S(1)}, u32[]{:S(2)}, u32[]{:S(2)}) collective-permute-start(f32[72,640]{1,0:T(8,128)S(1)} %get-tuple-element.42), channel_id=1, source_target_pairs={{1,2},{2,1},{3,4},{4,3},{5,6},{6,5},{7,127},{9,10},{10,9},{11,12},... | collective-permute-start | bytes 552968 | tf_op jit(solution)/shard_map/ppermute | solution.py:380
  (4 other events, 3.3 us)
where the time goes:
time: 179 us; the launch traced here: 178 us
  Pallas kernels  61.1 us (34%)
  blocking collectives  49.9 us (28%)
  starting transfers between devices  26.5 us (15%)
  waiting for transfers between devices  25.1 us (14%)
  local copies, waits for them, and re-layouts  13.6 us (8%)
    all_to_all x1, blocking collectives, body(): lax.all_to_all(slots, ('gx', 'gy'), split_axis=0, concat_axis=0, tiled=True)  49.9 us
    pallas_call x1, Pallas kernels, body(): pl.pallas_call(pick_kernel, out_shape=jax.ShapeDtypeStruct((listed, 2, BY...  34.1 us
    ppermute x2, waiting for transfers between devices, exchange_x(): lax.ppermute(to_west, 'gx', west)  20.1 us
    pallas_call x6, Pallas kernels, call(): pl.pallas_call(kernel, out_shape=[jax.ShapeDtypeStruct(s, F32) for s in o...  18.2 us
    unnamed x38, local copies, waits for them, and re-layouts  13.5 us
    all_to_all x1, starting transfers between devices, body(): lax.all_to_all(sums, ('gx', 'gy'), split_axis=0, concat_axis=0, tiled=True)  11.5 us
    pallas_call x1, Pallas kernels, body(): pl.pallas_call(sums_kernel, grid_spec=pltpu.PrefetchScalarGridSpec(num_sc...  8.73 us
    ppermute x2, starting transfers between devices, exchange_x(): lax.ppermute(to_west, 'gx', west)  7.97 us
  transfers between devices with their start and end apart: 9, of which 5 were waited for; matrix products, arithmetic and copies ran while one was open for 0% of the time, Pallas kernels for 3%

commit v1 on v0

v1 whole, which is shorter than its diff:
```python
import functools

import jax
import jax.numpy as jnp
from jax import lax
from jax.experimental import pallas as pl
from jax.experimental.pallas import tpu as pltpu
from jax.sharding import PartitionSpec as P

BX = 128
BY = 16
BCOL = 4
BROW = 20
LEV = 24
ITERS = 4
STENCIL_SUM = 5.0
CORNER_WEIGHT = 0.25
LOWER_BOUND = 0.02
UPPER_BOUND = 2.0

F32 = jnp.float32
EXT = BROW + 4
OFF = 2
DEPTH = 2
WIDE = BCOL * BX + BX
PART = DEPTH * BY
STRIP = 2 * PART + 8
SENT = STRIP + 8
CHUNK = 4
MIB = 1 << 20
GAMMA = (UPPER_BOUND + LOWER_BOUND) / 2.0
SCALE = 4.0 * (2.0 / (UPPER_BOUND - LOWER_BOUND)) ** 2
OMEGAS = [2.0 / GAMMA]
for _ in range(1, ITERS):
    OMEGAS.append(1.0 / (GAMMA - OMEGAS[-1] / SCALE))


def call(kernel, out_shape, operands, scratch, vmem):
    spaces = [
        pl.BlockSpec(memory_space=pltpu.SMEM if a.dtype == jnp.int32 and a.ndim == 1 else pltpu.VMEM)
        for a in operands
    ]
    size = sum(a.size * a.dtype.itemsize for a in operands)
    return pl.pallas_call(
        kernel,
        out_shape=[jax.ShapeDtypeStruct(s, F32) for s in out_shape],
        in_specs=spaces,
        out_specs=[pl.BlockSpec(memory_space=pltpu.VMEM) for _ in out_shape],
        scratch_shapes=[pltpu.VMEM(s, F32) for s in scratch],
        compiler_params=pltpu.CompilerParams(vmem_limit_bytes=vmem * MIB),
        cost_estimate=pl.CostEstimate(flops=4000000, bytes_accessed=size, transcendentals=0),
    )(*operands)


def lanes(shape):
    return lax.broadcasted_iota(jnp.int32, shape, 1)


def rows(shape):
    return lax.broadcasted_iota(jnp.int32, shape, 0)


def pack(tiles, last):
    lane = lanes(tiles[0].shape)
    packed = jnp.zeros(tiles[0].shape, F32)
    for p, tile in enumerate(tiles):
        shift = (8 * p + 8 if last else 8 * p) % BX
        moved = pltpu.roll(tile, shift, 1) if shift else tile
        packed = jnp.where(lane // 8 == p, moved, packed)
    return packed


def unpack(packed, p, at):
    shift = (at - 8 * p) % BX
    return pltpu.roll(packed, shift, 1) if shift else packed


def side_tile(east, west, p):
    lane = lanes(east.shape)
    tile = jnp.where(lane < 8, unpack(east, p, 0), 0.0)
    return jnp.where(lane >= BX - 8, unpack(west, p, BX - 8), tile)


def turned(strip):
    lane = BX - 1 - lanes((strip.shape[0], BX))
    tiles = [strip[:, BX * q : BX * q + BX] for q in range(WIDE // BX)]
    tiles = [jnp.take_along_axis(tile, lane, axis=1) for tile in tiles]
    return jnp.concatenate([tiles[(BCOL - 1 - q) % (BCOL + 1)] for q in range(BCOL + 1)], axis=1)


def beside(value):
    return pltpu.roll(value, 1, 1) + pltpu.roll(value, WIDE - 1, 1)


def send(strip, message):
    message[0:STRIP, :] = strip[:, 0 : BCOL * BX]
    lane = lanes((8, BX))
    packed = [jnp.zeros((8, BX), F32) for _ in range(BCOL)]
    for g in range(STRIP // 8):
        tile = strip[8 * g : 8 * g + 8, BCOL * BX : WIDE]
        moved = pltpu.roll(tile, (8 + 16 * (g % 8)) % BX, 1)
        packed[g // 8] = jnp.where(lane // 16 == g % 8, moved, packed[g // 8])
    message[STRIP:SENT, :] = jnp.concatenate(packed, axis=1)


def receive(message, strip):
    strip[:, 0 : BCOL * BX] = message[0:STRIP, :]
    lane = lanes((8, BX))
    inside = (lane < 8) | (lane >= BX - 8)
    for g in range(STRIP // 8):
        tile = message[STRIP:SENT, BX * (g // 8) : BX * (g // 8) + BX]
        moved = pltpu.roll(tile, (BX - 8 - 16 * (g % 8)) % BX, 1)
        strip[8 * g : 8 * g + 8, BCOL * BX : WIDE] = jnp.where(inside, moved, 0.0)


def sums_kernel(thickness, blocks, tendencies, out, buffer, listed, staged, weights, sems, out_sems, list_sem):
    count = buffer.shape[0]
    ny = lax.axis_size("gy")
    me = lax.axis_index("gx") * ny + lax.axis_index("gy")
    listing = pltpu.make_async_copy(blocks, listed, list_sem)
    listing.start()

    def fetch(c):
        part = pl.ds(c * CHUNK, CHUNK)
        return pltpu.make_async_copy(tendencies.at[part], buffer.at[part], sems.at[c])

    def leave(n):
        index = listed[me * count + n]
        row, col = index // (BCOL * lax.axis_size("gx")), index % (BCOL * lax.axis_size("gx"))
        owner = col // BCOL * ny + row // BROW
        return pltpu.make_async_copy(staged.at[n], out.at[owner], out_sems.at[n])

    for c in range(count // CHUNK):
        fetch(c).start()
    for level in range(LEV):
        weights[level] = jnp.full((BY, BX), thickness[level], F32)
    listing.wait()

    def chunk(c, carry):
        fetch(c).wait()
        for pair in range(CHUNK // 2):
            totals = [None] * 4
            for level in range(LEV):
                weight = weights[level]
                for k in range(4):
                    n = c * CHUNK + 2 * pair + k // 2
                    term = weight * buffer[n, k % 2, level].astype(F32)
                    totals[k] = term if totals[k] is None else totals[k] + term
            for k in range(4):
                staged[c * CHUNK + 2 * pair + k // 2, k % 2] = totals[k]
            for k in range(2):
                leave(c * CHUNK + 2 * pair + k).start()
        return carry

    lax.fori_loop(0, count // CHUNK, chunk, 0)

    def finish(n, carry):
        leave(n).wait()
        return carry

    lax.fori_loop(0, count, finish, 0)


def prepare_kernel(mask, implicit, guess, fields, work):
    for q in range(BCOL):
        cols = slice(BX * q, BX * q + BX)
        m = mask[:, cols].astype(F32)
        work[q] = m * (STENCIL_SUM + implicit[:, cols]) + (1.0 - m)
        work[BCOL + q] = m * guess[:, cols]
    edge = jnp.zeros((OFF, BX), F32)
    for k in range(2):
        for p in range(BY):
            for q in range(BCOL):
                tile = work[BCOL * k + q, pl.ds(p, BROW, stride=BY), :]
                tile = jnp.concatenate([edge, tile, edge], axis=0)
                fields[k, p, :, BX * q : BX * q + BX] = tile


def place_kernel(loc, arrived, fields, right, f1_top, to_east, to_west, work):
    def put(slot, carry):
        index = loc[slot]
        row, col = (index >> 2) + OFF, index & 3
        work[col, pl.ds(row, BY, stride=EXT), :] = arrived[slot, 0]
        work[BCOL + col, pl.ds(row, BY, stride=EXT), :] = arrived[slot, 1]
        return carry

    lax.fori_loop(0, arrived.shape[0], put, 0, unroll=8)
    lane = lanes((EXT, BX))
    row = rows((EXT, BX))
    first, last = [], []
    for q in range(BCOL):
        cols = slice(BX * q, BX * q + BX)

        def part(component, p, at):
            value = work[BCOL * component + at, EXT * p : EXT * p + EXT, :]
            return jnp.where(fields[0, p, :, BX * at : BX * at + BX] > 1.0, value, 0.0)

        south = pltpu.roll(part(1, BY - 1, q), 1, 0)
        for p in range(BY):
            f0 = part(0, p, q)
            f1 = part(1, p, q)
            west = pltpu.roll(f0, 1, 1)
            edge = pltpu.roll(part(0, p, q - 1), 1, 1) if q else 0.0
            west = jnp.where(lane == 0, edge, west)
            value = (f0 - west) + (f1 - south)
            right[p, :, cols] = value
            south = f1
            if q == 0:
                first.append(value)
            if q == BCOL - 1:
                last.append(jnp.where(lane == BX - 5, pltpu.roll(f0, BX - 4, 1), value))
        f1_top[:, cols] = jnp.broadcast_to(south[OFF + BROW - 1 : OFF + BROW, :], (8, BX))
    f1_row = row == EXT - 1
    to_west[0:EXT, :] = jnp.where(f1_row, f1_top[0:1, 0:BX], pack(first, False))
    to_east[0:EXT, :] = jnp.where(f1_row, f1_top[0:1, BX * (BCOL - 1) : BX * BCOL], pack(last, True))
    for k in range(2):
        part_rows = slice(EXT * (k + 1), EXT * (k + 2))
        to_west[part_rows, :] = pack([fields[k, p, :, 0:BX] for p in range(BY)], False)
        to_east[part_rows, :] = pack([fields[k, p, :, BX * (BCOL - 1) :] for p in range(BY)], True)


def widen_kernel(
    flags, right, f1_top, mine, east, west, fields,
    r_wide, d_wide, x_wide, edges, first, second,
    tall, update, top, bottom, flipped,
):
    lane = lanes((EXT, BX))
    side = slice(BCOL * BX, WIDE)
    for k, wide in enumerate((d_wide, x_wide)):
        part = slice(EXT * (k + 1), EXT * (k + 2))
        for p in range(BY):
            wide[p, :, 0 : BCOL * BX] = fields[k, p]
            wide[p, :, side] = side_tile(east[part, :], west[part, :], p)
    for p in range(BY):
        x = x_wide[p]
        tall[p] = x + CORNER_WEIGHT * beside(x)
    for p in range(BY):
        below = tall[p - 1] if p > 0 else pltpu.roll(tall[BY - 1], 1, 0)
        above = tall[p + 1] if p + 1 < BY else pltpu.roll(tall[0], EXT - 1, 0)
        x = x_wide[p]
        minus = beside(x) + (below + above) - d_wide[p] * x
        r_wide[p, :, BX : BCOL * BX] = right[p, :, BX:] + minus[:, BX : BCOL * BX]
        fix = jnp.where(lane == 0, unpack(west[0:EXT, :], p, BX - 3), 0.0)
        r_wide[p, :, 0:BX] = right[p, :, 0:BX] - fix + minus[:, 0:BX]
        fix = jnp.where(lane == 0, unpack(mine[0:EXT, :], p, BX - 3), 0.0)
        r_wide[p, :, side] = side_tile(east[0:EXT, :], west[0:EXT, :], p) - fix + minus[:, side]
    lane = lanes((1, BX))
    tile = jnp.where(lane < 8, east[EXT - 1 : EXT, :], 0.0)
    tile = jnp.where(lane >= BX - 8, west[EXT - 1 : EXT, :], tile)
    f1 = jnp.concatenate([f1_top[0:1, :], tile], axis=1)
    t_top = tall[BY - 1, OFF + BROW - 1 : OFF + BROW, :]
    t_bottom = tall[0, OFF : OFF + 1, :]
    edges[0:1, :] = t_top - f1
    edges[1:2, :] = t_top
    edges[2:3, :] = t_bottom
    edges[3:8, :] = jnp.zeros((5, WIDE), F32)

    ends = (slice(0, 8), slice(EXT - 8, EXT))

    def ends_of(field, p):
        return jnp.concatenate([field[p, end, :] for end in ends], axis=0)

    def line(residual):
        lower = []
        for p in range(BY):
            lower.append(residual(p) * inverse[p] if p == 0 else (residual(p) + lower[-1]) * inverse[p])
        upper = [lower[-1]]
        for p in range(BY - 2, -1, -1):
            upper.append(lower[p] + inverse[p] * upper[-1])
        return upper[::-1]

    inverse = []
    for p in range(BY):
        d = ends_of(d_wide, p)
        inverse.append(jnp.where(d > 1.0, 1.0 / (d - inverse[-1] if p else d), 0.0))
    for p, s in enumerate(line(lambda p: ends_of(r_wide, p))):
        u = s * (1.0 / GAMMA)
        update[p] = u
        tall[p, 0:16, :] = u + CORNER_WEIGHT * beside(u)

    def after(p):
        below = tall[p - 1, 0:16, :] if p > 0 else pltpu.roll(tall[BY - 1, 0:16, :], 1, 0)
        above = tall[p + 1, 0:16, :] if p + 1 < BY else pltpu.roll(tall[0, 0:16, :], 15, 0)
        u = update[p]
        return ends_of(r_wide, p) + (beside(u) + (below + above) - ends_of(d_wide, p) * u)

    smoothed = line(after)
    behind = OFF + DEPTH, 16 - OFF - DEPTH - 1
    pick = [(0, behind[0], bottom), (BY - 1, behind[1], top)]
    for k, wide in enumerate((r_wide, d_wide)):
        for p in range(BY):
            rows_at = slice(PART * k + DEPTH * p, PART * k + DEPTH * p + DEPTH)
            top[rows_at, :] = wide[p, OFF + BROW - DEPTH : OFF + BROW, :]
            bottom[rows_at, :] = wide[p, OFF : OFF + DEPTH, :]
    at = 2 * PART
    for p, n, strip in pick:
        u = update[p, n : n + 1, :]
        strip[at : at + 1, :] = u
        strip[at + 1 : at + 2, :] = OMEGAS[1] * smoothed[p][n : n + 1, :] + (GAMMA * OMEGAS[1] - 1.0) * u
        strip[at + 4 : STRIP, :] = jnp.zeros((STRIP - at - 4, WIDE), F32)
    top[at + 2 : at + 3, :] = edges[0:1, :]
    top[at + 3 : at + 4, :] = x_wide[BY - 1, OFF + BROW - 1 : OFF + BROW, :]
    bottom[at + 2 : at + 3, :] = t_bottom
    bottom[at + 3 : at + 4, :] = x_wide[0, OFF : OFF + 1, :]

    @pl.when(flags[1] == 1)
    def _():
        for k in range(2):
            for r in range(PART):
                flipped[PART * k + r : PART * k + r + 1, :] = top[PART * (k + 1) - 1 - r : PART * (k + 1) - r, :]
        flipped[at:STRIP, :] = top[at:STRIP, :]
        flipped[at + 2 : at + 3, :] = edges[1:2, :]
        flipped[...] = turned(flipped[...])
        send(bottom, first)
        send(flipped, second)

    @pl.when((flags[0] == 1) & (flags[1] == 0))
    def _():
        send(bottom, first)
        send(top, second)

    @pl.when(flags[0] == 0)
    def _():
        send(top, first)
        send(bottom, second)


def solve_kernel(
    flags, loc, r_wide, d_wide, x_wide, edges, first, second,
    solution, residual, slots,
    r_all, d_all, inverse, f_all, t_all, u_all, g_all, natural, south, north,
):
    @pl.when(flags[0] == 1)
    def _():
        receive(first, south)
        receive(second, north)

    @pl.when(flags[0] == 0)
    def _():
        receive(second, south)
        receive(first, north)

    row = rows((EXT, WIDE))
    previous = jnp.zeros((EXT, WIDE), F32)
    for k, (field, out) in enumerate(((r_wide, r_all), (d_wide, d_all))):
        for p in range(BY):
            part = slice(PART * k + DEPTH * p, PART * k + DEPTH * p + DEPTH)
            out[p] = field[p]
            out[p, 0:OFF, :] = south[part, :]
            out[p, OFF + BROW : EXT, :] = north[part, :]
    for p in range(BY):
        d = d_all[p]
        previous = jnp.where(d > 1.0, 1.0 / (d - previous), 0.0)
        inverse[p] = previous
    at = 2 * PART
    upward = jnp.where(flags[1] == 1, edges[1:2, :], edges[0:1, :])
    fix = jnp.where(row == OFF, south[at + 2 : at + 3, :], 0.0)
    r_all[0] = r_all[0] + jnp.where(row == OFF + BROW, upward, fix)
    fix = jnp.where(row == OFF + BROW - 1, north[at + 2 : at + 3, :], 0.0)
    r_all[BY - 1] = r_all[BY - 1] + jnp.where(row == OFF - 1, edges[2:3, :], fix)

    def gathered(p, k):
        below = t_all[p - 1] if p > 0 else pltpu.roll(t_all[BY - 1], 1, 0)
        above = t_all[p + 1] if p + 1 < BY else pltpu.roll(t_all[0], EXT - 1, 0)
        if k <= 2:
            at_k = slice(at + k - 1, at + k)
            if p == 0:
                u = south[at_k, :]
                below = jnp.where(row == 0, u + CORNER_WEIGHT * beside(u), below)
            if p == BY - 1:
                u = north[at_k, :]
                above = jnp.where(row == EXT - 1, u + CORNER_WEIGHT * beside(u), above)
        return r_all[p] + (below + above)

    for k, omega in enumerate(OMEGAS):
        f = None
        for p in range(BY):
            if k > 0:
                r = gathered(p, k)
                r_all[p] = r
            else:
                r = r_all[p]
            f = (r if f is None else r + f) * inverse[p]
            f_all[p] = f
        s = None
        for p in reversed(range(BY)):
            s = f_all[p] if s is None else f_all[p] + inverse[p] * s
            if k == 0:
                u = s * (1.0 / GAMMA)
            else:
                u = omega * s + (GAMMA * omega - 1.0) * u_all[k - 1, p]
            u_all[k, p] = u
            h = beside(u)
            t_all[p] = u + CORNER_WEIGHT * h
            r_all[p] = r_all[p] + (h - d_all[p] * u)
    for p in range(BY):
        r = jnp.where(d_all[p] > 1.0, gathered(p, ITERS), 0.0)
        start = x_wide[p]
        if p == 0:
            start = jnp.where(row == OFF + BROW, north[at + 3 : at + 4, :], start)
        x = start + ((u_all[0, p] + u_all[1, p]) + (u_all[2, p] + u_all[3, p]))
        f_all[p] = x
        for q in range(BCOL):
            cols = slice(BX * q, BX * q + BX)
            natural[q, pl.ds(p, BROW, stride=BY), :] = x[OFF : OFF + BROW, cols]
            natural[BCOL + q, pl.ds(p, BROW, stride=BY), :] = r[OFF : OFF + BROW, cols]
    for q in range(BCOL):
        cols = slice(BX * q, BX * q + BX)
        solution[:, cols] = natural[q]
        residual[:, cols] = natural[BCOL + q]
    for p in range(BY):
        x = f_all[p]
        ocean = d_all[p] > 1.0
        above = f_all[p + 1] if p + 1 < BY else pltpu.roll(f_all[0], EXT - 1, 0)
        zonal = jnp.where(ocean, pltpu.roll(x, WIDE - 1, 1) - x, 0.0)
        meridional = jnp.where(ocean, above - x, 0.0)
        for q in range(BCOL):
            cols = slice(BX * q, BX * q + BX)
            g_all[q, EXT * p : EXT * p + EXT, :] = zonal[:, cols]
            g_all[BCOL + q, EXT * p : EXT * p + EXT, :] = meridional[:, cols]

    def take(slot, carry):
        index = loc[slot]
        row, col = (index >> 2) + OFF, index & 3
        slots[slot, 0] = g_all[col, pl.ds(row, BY, stride=EXT), :]
        slots[slot, 1] = g_all[BCOL + col, pl.ds(row, BY, stride=EXT), :]
        return carry

    lax.fori_loop(0, slots.shape[0], take, 0, unroll=8)


def pick_kernel(dst, slots, out, sems):
    copies = [
        pltpu.make_async_copy(slots.at[dst[n]], out.at[n], sems.at[n]) for n in range(out.shape[0])
    ]
    for copy in copies:
        copy.start()
    for copy in copies:
        copy.wait()


def body(tendencies, thickness, ocean_blocks, land_mask, implicit_term, first_guess):
    nx = lax.axis_size("gx")
    ny = lax.axis_size("gy")
    gx = lax.axis_index("gx")
    gy = lax.axis_index("gy")
    devices = nx * ny
    listed = tendencies.shape[0]
    me = gx * ny + gy
    block_cols = BCOL * nx
    block_row = ocean_blocks // block_cols
    block_col = ocean_blocks % block_cols
    owner = block_col // BCOL * ny + block_row // BROW
    local = block_row % BROW * BCOL + block_col % BCOL
    dst = lax.dynamic_slice_in_dim(owner, me * listed, listed)
    loc = jnp.min(jnp.where(owner == me, local, BROW * BCOL).reshape(devices, listed), axis=1)
    flags = jnp.stack([gy % 2, (gy == ny - 1).astype(jnp.int32)]).astype(jnp.int32)

    east = [(i, (i + 1) % nx) for i in range(nx)]
    west = [(j, i) for i, j in east]
    swap_a, swap_b = [], []
    for i in range(nx):
        for j in range(ny):
            swap_a.append((i * ny + j, i * ny + (j ^ 1)))
            if j == ny - 1:
                swap_b.append((i * ny + j, (nx - 1 - i) * ny + j))
            elif j > 0:
                swap_b.append((i * ny + j, i * ny + (j + 1 if j % 2 else j - 1)))

    def exchange_x(to_east, to_west):
        return lax.ppermute(to_west, "gx", west), lax.ppermute(to_east, "gx", east)

    def exchange_y(first, second):
        return lax.ppermute(first, ("gx", "gy"), swap_a), lax.ppermute(second, ("gx", "gy"), swap_b)

    hbm = pl.BlockSpec(memory_space=pltpu.HBM)
    sums = pl.pallas_call(
        sums_kernel,
        out_shape=jax.ShapeDtypeStruct((devices, 2, BY, BX), F32),
        in_specs=[pl.BlockSpec(memory_space=pltpu.SMEM), hbm, hbm],
        out_specs=hbm,
        scratch_shapes=[
            pltpu.VMEM(tendencies.shape, tendencies.dtype),
            pltpu.SMEM(ocean_blocks.shape, jnp.int32),
            pltpu.VMEM((listed, 2, BY, BX), F32),
            pltpu.VMEM((LEV, BY, BX), F32),
            pltpu.SemaphoreType.DMA((listed // CHUNK,)),
            pltpu.SemaphoreType.DMA((listed,)),
            pltpu.SemaphoreType.DMA,
        ],
        compiler_params=pltpu.CompilerParams(vmem_limit_bytes=58 * MIB),
    )(thickness, ocean_blocks, tendencies)
    arrived = lax.all_to_all(sums, ("gx", "gy"), split_axis=0, concat_axis=0, tiled=True)

    own = (BY, EXT, BCOL * BX)
    full = (BY, EXT, WIDE)
    strip = (STRIP, WIDE)
    sent = (SENT, BCOL * BX)
    sums, land_mask, implicit_term, first_guess = lax.optimization_barrier(
        (sums, land_mask, implicit_term, first_guess)
    )
    (fields,) = call(
        prepare_kernel,
        [(2, *own)],
        [land_mask, implicit_term, first_guess],
        [(2 * BCOL, BROW * BY, BX)],
        6,
    )
    right, f1_top, to_east, to_west = call(
        place_kernel,
        [own, (8, BCOL * BX), (3 * EXT, BX), (3 * EXT, BX)],
        [loc, arrived, fields],
        [(2 * BCOL, BY * EXT, BX)],
        8,
    )
    r_wide, d_wide, x_wide, edges, first, second = call(
        widen_kernel,
        [full, full, full, (8, WIDE), sent, sent],
        [flags, right, f1_top, to_east, *exchange_x(to_east, to_west), fields],
        [full, (BY, 16, WIDE), strip, strip, strip],
        12,
    )
    solution, residual, slots = call(
        solve_kernel,
        [(BROW * BY, BCOL * BX), (BROW * BY, BCOL * BX), (devices, 2, BY, BX)],
        [flags, loc, r_wide, d_wide, x_wide, edges, *exchange_y(first, second)],
        [
            full,
            full,
            full,
            full,
            full,
            (ITERS, *full),
            (2 * BCOL, BY * EXT, BX),
            (2 * BCOL, BROW * BY, BX),
            strip,
            strip,
        ],
        20,
    )
    returned = lax.all_to_all(slots, ("gx", "gy"), split_axis=0, concat_axis=0, tiled=True)
    gradient_blocks = pl.pallas_call(
        pick_kernel,
        out_shape=jax.ShapeDtypeStruct((listed, 2, BY, BX), F32),
        in_specs=[pl.BlockSpec(memory_space=pltpu.SMEM), pl.BlockSpec(memory_space=pltpu.VMEM)],
        out_specs=pl.BlockSpec(memory_space=pl.ANY),
        scratch_shapes=[pltpu.SemaphoreType.DMA((listed,))],
        compiler_params=pltpu.CompilerParams(vmem_limit_bytes=4 * MIB),
    )(dst, returned)
    return solution, residual, gradient_blocks


def solution(mesh):
    placed = (
        P(("gx", "gy"), None, None, None, None),
        P(),
        P(),
        P("gy", "gx"),
        P("gy", "gx"),
        P("gy", "gx"),
    )
    return jax.shard_map(
        body,
        mesh=mesh,
        in_specs=placed,
        out_specs=(P("gy", "gx"), P("gy", "gx"), P(("gx", "gy"), None, None, None)),
        check_vma=False,
    )
```

time: 179 us -> 119 us (0.66)
  blocking collectives: 49.9 us -> 0 us
  Pallas kernels: 61.1 us -> 23.1 us
  waiting for transfers between devices: 25.1 us -> 60.3 us
  local copies, waits for them, and re-layouts: 13.6 us -> 2.2 us
  starting transfers between devices: 26.5 us -> 31.3 us
    all_to_all x1 -> x0, blocking collectives: 49.9 us -> none  [body(): lax.all_to_all(slots, ('gx', 'gy'), split_axis=0, concat_axis=0, tiled=True)]
    pallas_call x1, Pallas kernels: 34.1 us -> 2.05 us  [body(): pl.pallas_call(pick_kernel, out_shape=jax.ShapeDtypeStruct((listed, 2, BY...]
    all_to_all x0 -> x1, waiting for transfers between devices: none -> 28.5 us  [body(): lax.all_to_all(slots, ('gx', 'gy'), split_axis=0, concat_axis=0, tiled=True)]
    all_to_all x1, waiting for transfers between devices: 0.01 us -> 27.2 us  [body(): lax.all_to_all(sums, ('gx', 'gy'), split_axis=0, concat_axis=0, tiled=True)]
    ppermute x2 -> x1, waiting for transfers between devices: 20.1 us -> 1.56 us  [exchange_x(): lax.ppermute(to_west, 'gx', west)]
    all_to_all x0 -> x1, starting transfers between devices: none -> 16.3 us  [body(): lax.all_to_all(slots, ('gx', 'gy'), split_axis=0, concat_axis=0, tiled=True)]
    unnamed x38 -> x10, local copies, waits for them, and re-layouts: 13.5 us -> 1.36 us
    ppermute x2 -> x1, starting transfers between devices: 7.97 us -> 1.37 us  [exchange_x(): lax.ppermute(to_west, 'gx', west)]
  transfers between devices with their start and end apart: 9 -> 6, of which waited for: 5 -> 4; matrix products, arithmetic and copies ran while one was open for 0% -> 1% of each run, Pallas kernels for 3% -> 1%
where the time goes in v1:
time: 119 us
  waiting for transfers between devices  60.3 us (51%)
  starting transfers between devices  31.3 us (26%)
  Pallas kernels  23.1 us (19%)
  local copies, waits for them, and re-layouts  2.2 us (2%)
    all_to_all x1, waiting for transfers between devices, body(): lax.all_to_all(slots, ('gx', 'gy'), split_axis=0, concat_axis=0, tiled=True)  28.5 us
    all_to_all x1, waiting for transfers between devices, body(): lax.all_to_all(sums, ('gx', 'gy'), split_axis=0, concat_axis=0, tiled=True)  27.2 us
    all_to_all x1, starting transfers between devices, body(): lax.all_to_all(slots, ('gx', 'gy'), split_axis=0, concat_axis=0, tiled=True)  16.3 us
    pallas_call x4, Pallas kernels, call(): pl.pallas_call(kernel, out_shape=[jax.ShapeDtypeStruct(s, F32) for s in o...  14.1 us
    all_to_all x1, starting transfers between devices, body(): lax.all_to_all(sums, ('gx', 'gy'), split_axis=0, concat_axis=0, tiled=True)  12 us
    pallas_call x1, Pallas kernels, body(): pl.pallas_call(sums_kernel, out_shape=jax.ShapeDtypeStruct((devices, 2, B...  7.03 us
    ppermute x1, waiting for transfers between devices, exchange_y(): lax.ppermute(first, ('gx', 'gy'), swap_a)  2.99 us
  transfers between devices with their start and end apart: 6, of which 4 were waited for; matrix products, arithmetic and copies ran while one was open for 1% of the time, Pallas kernels for 1%

profile of v1, /device:TPU:1, one launch (start us, length us, event | category | flops | bytes accessed | tf_op | source)
XLA Modules:
  0.0 118.6 jit_solution(10123101864865481052)
XLA Ops:
  0.6 7.0 %shard_map.85 = f32[128,2,16,128]{3,2,1,0:T(8,128)} custom-call(f32[24]{0:T(128)} %thickness.1, s32[8192]{0:T(1024)} %blocks.1, bf16[64,2,24,16,128]{4,3,2,1,0:T(8,128)(2,1)} %tendencies.1), custom_call_target="tpu_custom_call" | custom-call | tf_op jit(solution)/shard_map/pallas_call | solution.py:477
  7.7 0.0 copy-start.4
  7.7 0.0 copy-start.3
  7.7 12.0 %all-to-all-start = ((f32[128,2,16,128]{3,2,1,0:T(8,128)}), f32[128,2,16,128]{3,2,1,0:T(8,128)}, u32[]{:S(2)}, u32[]{:S(2)}) async-start(f32[128,2,16,128]{3,2,1,0:T(8,128)} %shard_map.85), calls=%async_computation | async-start | bytes 4194304 | tf_op jit(solution)/shard_map/all_to_all | solution.py:493
  19.7 0.7 fusion.4
  20.4 0.1 reshape.9
  20.5 0.1 reduce_min.9.loc
  20.6 0.8 shard_map.86.fields
  21.4 27.2 %all-to-all-done.arrived = f32[128,2,16,128]{3,2,1,0:T(8,128)} async-done(((f32[128,2,16,128]{3,2,1,0:T(8,128)}), f32[128,2,16,128]{3,2,1,0:T(8,128)}, u32[]{:S(2)}, u32[]{:S(2)}) %all-to-all-start) | async-done | bytes 2097184 | tf_op jit(solution)/shard_map/all_to_all | solution.py:493
  48.6 3.0 %shard_map.87 = (f32[16,24,512]{2,1,0:T(8,128)S(1)}, f32[8,512]{1,0:T(8,128)S(1)}, f32[72,128]{1,0:T(8,128)S(1)}, f32[72,128]{1,0:T(8,128)S(1)}) custom-call(s32[128]{0:T(128)S(1)} %reduce_min.9.loc, f32[128,2,16,128]{3,2,1,0:T(8,128)} %all-to-all-done.arrived, f32[2,16,24,512]{3,2,1,0:T(8,128)S(1)} %shard_map.86.fields), custom_call_target="tpu_custom_call" | custom-call | flops 4000000 | bytes 3670528 | tf_op jit(solution)/shard_map/pallas_call | solution.py:44
  51.6 1.4 %collective-permute-start = (f32[72,128]{1,0:T(8,128)S(1)}, f32[72,128]{1,0:T(8,128)S(1)}, u32[]{:S(2)}, u32[]{:S(2)}) collective-permute-start(f32[72,128]{1,0:T(8,128)S(1)} %get-tuple-element.25), channel_id=1, source_target_pairs={{8,0},{16,8},{24,16},{32,24},{40,32},{48,40},{56,48},{64,56},{72,6... | collective-permute-start | bytes 110600 | tf_op jit(solution)/shard_map/ppermute | solution.py:471
  53.0 0.4 collective-permute-start.1
  53.4 0.1 pad_add_fusion.flags
  53.5 1.6 %collective-permute-done.east = f32[72,128]{1,0:T(8,128)S(1)} collective-permute-done((f32[72,128]{1,0:T(8,128)S(1)}, f32[72,128]{1,0:T(8,128)S(1)}, u32[]{:S(2)}, u32[]{:S(2)}) %collective-permute-start) | collective-permute-done | bytes 36896 | tf_op jit(solution)/shard_map/ppermute | solution.py:471
  55.1 3.4 %shard_map.88 = (f32[16,24,640]{2,1,0:T(8,128)S(1)}, f32[16,24,640]{2,1,0:T(8,128)S(1)}, f32[16,24,640]{2,1,0:T(8,128)S(1)}, f32[8,640]{1,0:T(8,128)S(1)}, f32[80,512]{1,0:T(8,128)S(1)}, /*index=5*/f32[80,512]{1,0:T(8,128)S(1)}) custom-call(s32[2]{0:T(128)S(1)} %pad_add_fusion.flags, f32[16,24,512]{2,1,0:T(8,128)S(1)} %get-tuple-element.22.right, ...), custom_call_target="tpu_custom_call" | custom-call | flops 4000000 | bytes 2486280 | tf_op jit(solution)/shard_map/pallas_call | solution.py:44
  58.5 0.6 collective-permute-start.2
  59.1 0.7 collective-permute-start.3
  59.8 3.0 %collective-permute-done.2.first = f32[80,512]{1,0:T(8,128)S(1)} collective-permute-done((f32[80,512]{1,0:T(8,128)S(1)}, f32[80,512]{1,0:T(8,128)S(1)}, u32[]{:S(2)}, u32[]{:S(2)}) %collective-permute-start.2) | collective-permute-done | bytes 163872 | tf_op jit(solution)/shard_map/ppermute | solution.py:474
  62.7 6.9 %shard_map.89 = (f32[320,512]{1,0:T(8,128)}, f32[320,512]{1,0:T(8,128)}, f32[128,2,16,128]{3,2,1,0:T(8,128)S(1)}) custom-call(s32[2]{0:T(128)S(1)} %pad_add_fusion.flags, s32[128]{0:T(128)S(1)} %reduce_min.9.loc, f32[16,24,640]{2,1,0:T(8,128)S(1)} %get-tuple-element.26.r_wide, f32[16,24,640]{2,1,0:T(8,128)S(1)} %get-tuple-element.27.d_wide, ...), custom_call_target="tpu_custom_call" | custom-call | flops 4000000 | bytes 3297800 | tf_op jit(solution)/shard_map/pallas_call | solution.py:44
  69.6 1.3 %copy-done = f32[128,2,16,128]{3,2,1,0:T(8,128)} copy-done((f32[128,2,16,128]{3,2,1,0:T(8,128)}, f32[128,2,16,128]{3,2,1,0:T(8,128)S(1)}, u32[]{:S(2)}) %copy-start) | copy-done | bytes 2097176
  70.9 16.3 %all-to-all-start.1 = ((f32[128,2,16,128]{3,2,1,0:T(8,128)}), f32[128,2,16,128]{3,2,1,0:T(8,128)S(1)}, u32[]{:S(2)}, u32[]{:S(2)}) async-start(f32[128,2,16,128]{3,2,1,0:T(8,128)} %copy-done), calls=%async_computation.1 | async-start | bytes 4194304 | tf_op jit(solution)/shard_map/all_to_all | solution.py:541
  87.2 0.8 dynamic_slice.3.dst
  88.0 28.5 %all-to-all-done.1.slots = f32[128,2,16,128]{3,2,1,0:T(8,128)S(1)} async-done(((f32[128,2,16,128]{3,2,1,0:T(8,128)}), f32[128,2,16,128]{3,2,1,0:T(8,128)S(1)}, u32[]{:S(2)}, u32[]{:S(2)}) %all-to-all-start.1) | async-done | bytes 2097184 | tf_op jit(solution)/shard_map/all_to_all | solution.py:541
  116.5 2.1 %shard_map.90 = f32[64,2,16,128]{3,2,1,0:T(8,128)} custom-call(s32[64]{0:T(128)S(1)} %dynamic_slice.3.dst, f32[128,2,16,128]{3,2,1,0:T(8,128)S(1)} %all-to-all-done.1.slots), custom_call_target="tpu_custom_call" | custom-call | tf_op jit(solution)/shard_map/pallas_call | solution.py:542
  (9 shorter events, 0.0 us)
Async XLA Ops:
  7.7 12.0 %copy-start.4 = (s32[8192]{0:T(1024)S(1)}, s32[8192]{0:T(1024)}, u32[]{:S(2)}) copy-start(s32[8192]{0:T(1024)} %blocks.1) | copy-start | bytes 98308
  7.7 12.9 %copy-start.1 = (s32[320,512]{1,0:T(8,128)S(1)}, s32[320,512]{1,0:T(8,128)}, u32[]{:S(2)}) copy-start(s32[320,512]{1,0:T(8,128)} %mask) | copy-start | bytes 1966084
  7.7 12.9 %copy-start.2 = (f32[320,512]{1,0:T(8,128)S(1)}, f32[320,512]{1,0:T(8,128)}, u32[]{:S(2)}) copy-start(f32[320,512]{1,0:T(8,128)} %implicit) | copy-start | bytes 1966084
  7.7 12.9 %copy-start.3 = (f32[320,512]{1,0:T(8,128)S(1)}, f32[320,512]{1,0:T(8,128)}, u32[]{:S(2)}) copy-start(f32[320,512]{1,0:T(8,128)} %guess) | copy-start | bytes 1966084
  7.7 40.9 %all-to-all-start = ((f32[128,2,16,128]{3,2,1,0:T(8,128)}), f32[128,2,16,128]{3,2,1,0:T(8,128)}, u32[]{:S(2)}, u32[]{:S(2)}) async-start(f32[128,2,16,128]{3,2,1,0:T(8,128)} %shard_map.85), calls=%async_computation | async-start | bytes 4194304 | tf_op jit(solution)/shard_map/all_to_all | solution.py:493
  51.6 3.5 %collective-permute-start = (f32[72,128]{1,0:T(8,128)S(1)}, f32[72,128]{1,0:T(8,128)S(1)}, u32[]{:S(2)}, u32[]{:S(2)}) collective-permute-start(f32[72,128]{1,0:T(8,128)S(1)} %get-tuple-element.25), channel_id=1, source_target_pairs={{8,0},{16,8},{24,16},{32,24},{40,32},{48,40},{56,48},{64,56},{72,6... | collective-permute-start | bytes 110600 | tf_op jit(solution)/shard_map/ppermute | solution.py:471
  53.0 2.1 %collective-permute-start.1 = (f32[72,128]{1,0:T(8,128)S(1)}, f32[72,128]{1,0:T(8,128)S(1)}, u32[]{:S(2)}, u32[]{:S(2)}) collective-permute-start(f32[72,128]{1,0:T(8,128)S(1)} %get-tuple-element.24.mine), channel_id=1, source_target_pairs={{0,8},{8,16},{16,24},{24,32},{32,40},{40,48},{48,56},{56,64},{64,7... | collective-permute-start | bytes 110600 | tf_op jit(solution)/shard_map/ppermute | solution.py:471
  58.5 4.2 %collective-permute-start.2 = (f32[80,512]{1,0:T(8,128)S(1)}, f32[80,512]{1,0:T(8,128)S(1)}, u32[]{:S(2)}, u32[]{:S(2)}) collective-permute-start(f32[80,512]{1,0:T(8,128)S(1)} %get-tuple-element.30), channel_id=1, source_target_pairs={{0,1},{1,0},{2,3},{3,2},{4,5},{5,4},{6,7},{7,6},{8,9},{9,8},{10,11... | collective-permute-start | bytes 491528 | tf_op jit(solution)/shard_map/ppermute | solution.py:474
  59.1 3.7 %collective-permute-start.3 = (f32[80,512]{1,0:T(8,128)S(1)}, f32[80,512]{1,0:T(8,128)S(1)}, u32[]{:S(2)}, u32[]{:S(2)}) collective-permute-start(f32[80,512]{1,0:T(8,128)S(1)} %get-tuple-element.31), channel_id=1, source_target_pairs={{1,2},{2,1},{3,4},{4,3},{5,6},{6,5},{7,127},{9,10},{10,9},{11,12},... | collective-permute-start | bytes 491528 | tf_op jit(solution)/shard_map/ppermute | solution.py:474
  69.6 1.3 %copy-start = (f32[128,2,16,128]{3,2,1,0:T(8,128)}, f32[128,2,16,128]{3,2,1,0:T(8,128)S(1)}, u32[]{:S(2)}) copy-start(f32[128,2,16,128]{3,2,1,0:T(8,128)S(1)} %get-tuple-element.34) | copy-start | bytes 6291460
  70.9 45.6 %all-to-all-start.1 = ((f32[128,2,16,128]{3,2,1,0:T(8,128)}), f32[128,2,16,128]{3,2,1,0:T(8,128)S(1)}, u32[]{:S(2)}, u32[]{:S(2)}) async-start(f32[128,2,16,128]{3,2,1,0:T(8,128)} %copy-done), calls=%async_computation.1 | async-start | bytes 4194304 | tf_op jit(solution)/shard_map/all_to_all | solution.py:541

commit v2 on v1

v2 whole, which is shorter than its diff:
```python
import functools

import jax
import jax.numpy as jnp
from jax import lax
from jax.experimental import pallas as pl
from jax.experimental.pallas import tpu as pltpu
from jax.sharding import PartitionSpec as P

BX = 128
BY = 16
BCOL = 4
BROW = 20
LEV = 24
ITERS = 4
STENCIL_SUM = 5.0
CORNER_WEIGHT = 0.25
LOWER_BOUND = 0.02
UPPER_BOUND = 2.0

F32 = jnp.float32
EXT = BROW + 4
OFF = 2
DEPTH = 1
WIDE = BCOL * BX + BX
PART = DEPTH * BY
SINGLE = 6
STRIP = 2 * PART + 8
SENT = STRIP
CHUNK = 4
MIB = 1 << 20
GAMMA = (UPPER_BOUND + LOWER_BOUND) / 2.0
SCALE = 4.0 * (2.0 / (UPPER_BOUND - LOWER_BOUND)) ** 2
OMEGAS = [2.0 / GAMMA]
for _ in range(1, ITERS):
    OMEGAS.append(1.0 / (GAMMA - OMEGAS[-1] / SCALE))


def call(kernel, out_shape, operands, scratch, vmem):
    spaces = [
        pl.BlockSpec(memory_space=pltpu.SMEM if a.dtype == jnp.int32 and a.ndim == 1 else pltpu.VMEM)
        for a in operands
    ]
    return pl.pallas_call(
        kernel,
        out_shape=[jax.ShapeDtypeStruct(s, F32) for s in out_shape],
        in_specs=spaces,
        out_specs=[pl.BlockSpec(memory_space=pltpu.VMEM) for _ in out_shape],
        scratch_shapes=[pltpu.VMEM(s, F32) for s in scratch],
        compiler_params=pltpu.CompilerParams(vmem_limit_bytes=vmem * MIB),
        cost_estimate=pl.CostEstimate(flops=1, bytes_accessed=1, transcendentals=0),
    )(*operands)


def lanes(shape):
    return lax.broadcasted_iota(jnp.int32, shape, 1)


def rows(shape):
    return lax.broadcasted_iota(jnp.int32, shape, 0)


def pack(tiles, last):
    lane = lanes(tiles[0].shape)
    packed = jnp.zeros(tiles[0].shape, F32)
    for p, tile in enumerate(tiles):
        shift = (8 * p + 8 if last else 8 * p) % BX
        moved = pltpu.roll(tile, shift, 1) if shift else tile
        packed = jnp.where(lane // 8 == p, moved, packed)
    return packed


def unpack(packed, p, at):
    shift = (at - 8 * p) % BX
    return pltpu.roll(packed, shift, 1) if shift else packed


def side_tile(east, west, p):
    lane = lanes(east.shape)
    tile = jnp.where(lane < 8, unpack(east, p, 0), 0.0)
    return jnp.where(lane >= BX - 8, unpack(west, p, BX - 8), tile)


def turned(strip):
    lane = BX - 1 - lanes((strip.shape[0], BX))
    tiles = [strip[:, BX * q : BX * q + BX] for q in range(WIDE // BX)]
    tiles = [jnp.take_along_axis(tile, lane, axis=1) for tile in tiles]
    return jnp.concatenate([tiles[(BCOL - 1 - q) % (BCOL + 1)] for q in range(BCOL + 1)], axis=1)


def beside(value):
    return pltpu.roll(value, 1, 1) + pltpu.roll(value, WIDE - 1, 1)


def send(strip, message):
    message[0 : 2 * PART, :] = strip[0 : 2 * PART, 0 : BCOL * BX]
    lane = lanes((8, BX))
    packed = jnp.zeros((8, BX), F32)
    for g in range(STRIP // 8):
        tile = strip[8 * g : 8 * g + 8, BCOL * BX : WIDE]
        packed = jnp.where(lane // 16 == g, pltpu.roll(tile, (8 + 16 * g) % BX, 1), packed)
    message[2 * PART : SENT, 0:BX] = packed
    for k in range(SINGLE):
        for q in range(BCOL):
            n = BCOL * k + q
            cols = slice(BX * (1 + n // 8), BX * (2 + n // 8))
            message[2 * PART + n % 8 : 2 * PART + n % 8 + 1, cols] = strip[
                2 * PART + k : 2 * PART + k + 1, BX * q : BX * q + BX
            ]


def receive(message, strip):
    strip[0 : 2 * PART, 0 : BCOL * BX] = message[0 : 2 * PART, :]
    lane = lanes((8, BX))
    inside = (lane < 8) | (lane >= BX - 8)
    packed = message[2 * PART : SENT, 0:BX]
    for g in range(STRIP // 8):
        moved = pltpu.roll(packed, (BX - 8 - 16 * g) % BX, 1)
        strip[8 * g : 8 * g + 8, BCOL * BX : WIDE] = jnp.where(inside, moved, 0.0)
    for k in range(SINGLE):
        for q in range(BCOL):
            n = BCOL * k + q
            cols = slice(BX * (1 + n // 8), BX * (2 + n // 8))
            strip[2 * PART + k : 2 * PART + k + 1, BX * q : BX * q + BX] = message[
                2 * PART + n % 8 : 2 * PART + n % 8 + 1, cols
            ]


def sums_kernel(
    thickness, blocks, tendencies, out, buffer, listed, staged, edges, weights, sems, out_sems, other_sems
):
    count = buffer.shape[0]
    nx, ny = lax.axis_size("gx"), lax.axis_size("gy")
    me = lax.axis_index("gx") * ny + lax.axis_index("gy")
    listing = pltpu.make_async_copy(blocks, listed, other_sems.at[0])
    listing.start()

    def fetch(c):
        part = pl.ds(c * CHUNK, CHUNK)
        return pltpu.make_async_copy(tendencies.at[part], buffer.at[part], sems.at[c])

    def leave(n, owner):
        return pltpu.make_async_copy(staged.at[n], out.at[owner, pl.ds(0, 2 * BY // 4)], out_sems.at[n])

    row16, lane16 = rows((BY, BX)), lanes((BY, BX))
    row4 = rows((4, BX))

    for c in range(count // CHUNK):
        fetch(c).start()
    for level in range(LEV):
        weights[level] = jnp.full((BY, BX), thickness[level], F32)
    listing.wait()

    def chunk(c, carry):
        fetch(c).wait()
        for pair in range(CHUNK // 2):
            totals = [None] * 4
            for level in range(LEV):
                weight = weights[level]
                for k in range(4):
                    n = c * CHUNK + 2 * pair + k // 2
                    term = weight * buffer[n, k % 2, level].astype(F32)
                    totals[k] = term if totals[k] is None else totals[k] + term
            for k in range(2):
                n = c * CHUNK + 2 * pair + k
                index = listed[me * count + n]
                row, col = lax.div(index, BCOL * nx), lax.rem(index, BCOL * nx)
                tile_row, tile_col, at = lax.div(row, BROW), lax.div(col, BCOL), lax.rem(col, BCOL)
                both = totals[2 * k : 2 * k + 2]
                for part in range(2):
                    staged[n, 4 * part : 4 * part + 4] = both[part].reshape(4, 4, BX)
                leave(n, tile_col * ny + tile_row).start()
                east_edge = at == BCOL - 1
                source = lane16 % 8 + jnp.where(east_edge, BX - 8, 0)
                line = []
                for value in both:
                    spread = jnp.take_along_axis(value, source, axis=1)
                    spread = jnp.where(lane16 // 8 == row16, spread, 0.0)
                    line.append(jnp.sum(spread, axis=0, keepdims=True))
                beside_col = lax.rem(tile_col + jnp.where(east_edge, 1, nx - 1), nx)
                slot = jnp.where((at == 0) | east_edge, beside_col * ny + tile_row, edges.shape[0] - 1)
                value = jnp.where(row4 % 2 == 0, line[0], line[1])
                edges[slot] = jnp.where(row4 // 2 == jnp.where(east_edge, 1, 0), value, edges[slot])
        return carry

    lax.fori_loop(0, count // CHUNK, chunk, 0)
    sides = pltpu.make_async_copy(edges.at[pl.ds(0, nx * ny)], out.at[:, 2 * BY // 4], other_sems.at[1])
    sides.start()

    def finish(n, carry):
        leave(n, 0).wait()
        return carry

    lax.fori_loop(0, count, finish, 0)
    sides.wait()


def prepare_kernel(mask, implicit, guess, fields, to_east, to_west, work):
    for q in range(BCOL):
        cols = slice(BX * q, BX * q + BX)
        m = mask[:, cols].astype(F32)
        work[q] = m * (STENCIL_SUM + implicit[:, cols]) + (1.0 - m)
        work[BCOL + q] = m * guess[:, cols]
    edge = jnp.zeros((OFF, BX), F32)
    for k in range(2):
        for p in range(BY):
            for q in range(BCOL):
                tile = work[BCOL * k + q, pl.ds(p, BROW, stride=BY), :]
                tile = jnp.concatenate([edge, tile, edge], axis=0)
                fields[k, p, :, BX * q : BX * q + BX] = tile
        part = slice(EXT * k, EXT * k + EXT)
        to_west[part, :] = pack([fields[k, p, :, 0:BX] for p in range(BY)], False)
        to_east[part, :] = pack([fields[k, p, :, BX * (BCOL - 1) :] for p in range(BY)], True)


def put_blocks(came, arrived, work, first_row, count, height, offset):
    row16, lane16 = rows((BY, BX)), lanes((BY, BX))
    spread = 8 * row16 + lane16 % 8

    def put(n, carry):
        block_row = jnp.clip(first_row + n, 0, BROW - 1)
        at_rows = pl.ds(n + offset, BY, stride=height)
        for col in range(BCOL):
            slot = came[block_row * BCOL + col]
            for part in range(2):
                value = arrived[slot, 4 * part : 4 * part + 4].reshape(BY, BX)
                work[(BCOL + 2) * part + col, at_rows, :] = value
        for side in range(2):
            slot = came[(BCOL + side) * BROW + block_row]
            for part in range(2):
                line = arrived[slot, 8, 2 * side + part : 2 * side + part + 1]
                value = jnp.take_along_axis(jnp.broadcast_to(line, (BY, BX)), spread, axis=1)
                work[(BCOL + 2) * part + BCOL + side, at_rows, :] = value
        return carry

    lax.fori_loop(0, count, put, 0, unroll=4)


def right_side(work, fields, east, west, parts, r_wide, d_wide, x_wide, inverse, tall):
    height = sum(high - low for low, high in parts)
    for k, wide in enumerate((d_wide, x_wide)):
        sides = [
            jnp.concatenate([side[EXT * k + low : EXT * k + high, :] for low, high in parts], axis=0)
            for side in (east, west)
        ]
        for p in range(BY):
            at = 0
            for low, high in parts:
                wide[p, at : at + high - low, 0 : BCOL * BX] = fields[k, p, low:high, :]
                at += high - low
            wide[p, :, BCOL * BX : WIDE] = side_tile(*sides, p)
    previous = None
    for p in range(BY):
        d = d_wide[p]
        previous = jnp.where(d > 1.0, 1.0 / (d if p == 0 else d - previous), 0.0)
        inverse[p] = previous
        x = x_wide[p]
        tall[p] = x + CORNER_WEIGHT * beside(x)
    lane = lanes((height, BX))

    def forcing(part, p):
        at = slice(height * p, height * p + height)
        tiles = [work[(BCOL + 2) * part + q, at, :] for q in range(BCOL + 2)]
        tiles[BCOL] = jnp.where(lane < BX // 2, tiles[BCOL], tiles[BCOL + 1])
        value = jnp.concatenate(tiles[: BCOL + 1], axis=1)
        return jnp.where(d_wide[p] > 1.0, value, 0.0)

    last = forcing(1, BY - 1)
    south = pltpu.roll(last, 1, 0)
    for p in range(BY):
        f0 = forcing(0, p)
        f1 = forcing(1, p) if p + 1 < BY else last
        below = tall[p - 1] if p > 0 else pltpu.roll(tall[BY - 1], 1, 0)
        above = tall[p + 1] if p + 1 < BY else pltpu.roll(tall[0], height - 1, 0)
        x = x_wide[p]
        minus_a = beside(x) + (below + above) - d_wide[p] * x
        r_wide[p] = (f0 - pltpu.roll(f0, 1, 1)) + (f1 - south) + minus_a
        south = f1
    return last


def right_kernel(
    came, arrived, fields, east, west,
    r_wide, d_wide, x_wide, inverse, edges,
    work, tall,
):
    put_blocks(came, arrived, work, 0, BROW, EXT, OFF)
    last = right_side(work, fields, east, west, ((0, EXT),), r_wide, d_wide, x_wide, inverse, tall)
    t_top = tall[BY - 1, OFF + BROW - 1 : OFF + BROW, :]
    edges[0:1, :] = t_top - last[OFF + BROW - 1 : OFF + BROW, :]
    edges[1:2, :] = t_top
    edges[2:3, :] = tall[0, OFF : OFF + 1, :]
    edges[3:8, :] = jnp.zeros((5, WIDE), F32)


def ends_kernel(
    flags, came, arrived, fields, east, west, first, second,
    work, r_wide, d_wide, x_wide, inverse, tall, update, top, bottom, flipped,
):
    put_blocks(came, arrived, work, -OFF, 8, 16, 0)
    put_blocks(came, arrived, work, EXT - 8 - OFF, 8, 16, 8)
    parts = ((0, 8), (EXT - 8, EXT))
    last = right_side(work, fields, east, west, parts, r_wide, d_wide, x_wide, inverse, tall)
    at = 2 * PART
    south, north = OFF, 16 - OFF - 1
    for k, wide in enumerate((r_wide, d_wide)):
        for p in range(BY):
            part = slice(PART * k + DEPTH * p, PART * k + DEPTH * p + DEPTH)
            top[part, :] = wide[p, north : north + DEPTH, :]
            bottom[part, :] = wide[p, south : south + DEPTH, :]
    t_top = tall[BY - 1, north : north + 1, :]
    top[at + 4 : at + 5, :] = t_top - jnp.where(flags[1] == 1, 0.0, last[north : north + 1, :])
    top[at + 5 : at + 6, :] = x_wide[BY - 1, north : north + 1, :]
    bottom[at + 4 : at + 5, :] = tall[0, south : south + 1, :]
    bottom[at + 5 : at + 6, :] = x_wide[0, south : south + 1, :]

    def line():
        lower = []
        for p in range(BY):
            r = r_wide[p] if p == 0 else r_wide[p] + lower[-1]
            lower.append(r * inverse[p])
        upper = [lower[-1]]
        for p in range(BY - 2, -1, -1):
            upper.append(lower[p] + inverse[p] * upper[-1])
        return upper[::-1]

    behind = ((0, south + 1, bottom), (BY - 1, north - 1, top))
    row = rows((16, WIDE))
    strips = (row == south) | (row == north)
    for k in range(2):
        for p, s in enumerate(line()):
            u = s * (1.0 / GAMMA) if k == 0 else OMEGAS[1] * s + (GAMMA * OMEGAS[1] - 1.0) * update[p]
            update[p] = u
            t = u + CORNER_WEIGHT * beside(u)
            tall[p] = t if k == 0 else jnp.where(strips, 0.0, t)
        for p in range(BY):
            below = tall[p - 1] if p > 0 else pltpu.roll(tall[BY - 1], 1, 0)
            above = tall[p + 1] if p + 1 < BY else pltpu.roll(tall[0], 15, 0)
            u = update[p]
            r_wide[p] = r_wide[p] + (beside(u) + (below + above) - d_wide[p] * u)
        for p, n, strip in behind:
            strip[at + k : at + k + 1, :] = update[p, n : n + 1, :]
    smoothed = line()
    element = None
    for p in reversed(range(BY)):
        d = d_wide[p]
        element = jnp.where(d > 1.0, 1.0 / (d if element is None else d - element), 0.0)
    for (p, n, strip), diagonal in zip(behind, (element, inverse[BY - 1])):
        strip[at + 2 : at + 3, :] = smoothed[p][n : n + 1, :]
        strip[at + 3 : at + 4, :] = diagonal[n : n + 1, :]
        strip[at + SINGLE : STRIP, :] = jnp.zeros((STRIP - at - SINGLE, WIDE), F32)

    @pl.when(flags[1] == 1)
    def _():
        for k in range(2):
            for r in range(PART):
                flipped[PART * k + r : PART * k + r + 1, :] = top[PART * (k + 1) - 1 - r : PART * (k + 1) - r, :]
        flipped[at:STRIP, :] = top[at:STRIP, :]
        top[...] = turned(flipped[...])

    @pl.when(flags[0] == 1)
    def _():
        send(bottom, first)
        send(top, second)

    @pl.when(flags[0] == 0)
    def _():
        send(top, first)
        send(bottom, second)


def solve_kernel(
    flags, loc, r_wide, d_wide, x_wide, inverse_own, edges, first, second,
    solution, residual, slots,
    r_all, d_all, inverse, f_all, t_all, u_all, g_all, natural, south, north, sems,
):
    @pl.when(flags[0] == 1)
    def _():
        receive(first, south)
        receive(second, north)

    @pl.when(flags[0] == 0)
    def _():
        receive(second, south)
        receive(first, north)

    row = rows((EXT, WIDE))
    for k, (field, out) in enumerate(((r_wide, r_all), (d_wide, d_all))):
        for p in range(BY):
            part = slice(PART * k + DEPTH * p, PART * k + DEPTH * p + DEPTH)
            out[p] = field[p]
            out[p, OFF - DEPTH : OFF, :] = south[part, :]
            out[p, OFF + BROW : OFF + BROW + DEPTH, :] = north[part, :]
    previous = None
    for p in range(BY):
        d = jnp.concatenate([d_all[p, 0:8, :], d_all[p, EXT - 8 : EXT, :]], axis=0)
        previous = jnp.where(d > 1.0, 1.0 / (d if p == 0 else d - previous), 0.0)
        inverse[p, 0:8, :] = previous[0:8, :]
        inverse[p, 8 : EXT - 8, :] = inverse_own[p, 8 : EXT - 8, :]
        inverse[p, EXT - 8 : EXT, :] = previous[8:16, :]
    at = 2 * PART
    upward = jnp.where(flags[1] == 1, edges[1:2, :], edges[0:1, :])
    fix = jnp.where(row == OFF, south[at + 4 : at + 5, :], 0.0)
    r_all[0] = r_all[0] + jnp.where(row == OFF + BROW, upward, fix)
    fix = jnp.where(row == OFF + BROW - 1, north[at + 4 : at + 5, :], 0.0)
    r_all[BY - 1] = r_all[BY - 1] + jnp.where(row == OFF - 1, edges[2:3, :], fix)

    def gathered(p, k):
        below = t_all[p - 1] if p > 0 else pltpu.roll(t_all[BY - 1], 1, 0)
        above = t_all[p + 1] if p + 1 < BY else pltpu.roll(t_all[0], EXT - 1, 0)
        if k < ITERS:
            at_k = slice(at + k - 1, at + k)
            if p == 0:
                u = south[at_k, :]
                below = jnp.where(row == OFF - 1, u + CORNER_WEIGHT * beside(u), below)
            if p == BY - 1:
                u = north[at_k, :]
                above = jnp.where(row == OFF + BROW, u + CORNER_WEIGHT * beside(u), above)
        return r_all[p] + (below + above)

    for k, omega in enumerate(OMEGAS):
        f = None
        for p in range(BY):
            if k > 0:
                r = gathered(p, k)
                r_all[p] = r
            else:
                r = r_all[p]
            f = (r if f is None else r + f) * inverse[p]
            f_all[p] = f
        s = None
        for p in reversed(range(BY)):
            s = f_all[p] if s is None else f_all[p] + inverse[p] * s
            if k == 0:
                u = s * (1.0 / GAMMA)
            else:
                u = omega * s + (GAMMA * omega - 1.0) * u_all[k - 1, p]
            u_all[k, p] = u
            h = beside(u)
            t_all[p] = u + CORNER_WEIGHT * h
            r_all[p] = r_all[p] + (h - d_all[p] * u)
        if k == 1:
            for strip, p, n in ((south, 0, OFF - 1), (north, BY - 1, OFF + BROW)):
                s = strip[at + 2 : at + 3, :] + strip[at + 3 : at + 4, :] * t_all[p, n : n + 1, :]
                u = OMEGAS[2] * s + (GAMMA * OMEGAS[2] - 1.0) * strip[at + 1 : at + 2, :]
                strip[at + 2 : at + 3, :] = u
    for p in range(BY):
        r = jnp.where(d_all[p] > 1.0, gathered(p, ITERS), 0.0)
        start = x_wide[p]
        if p == 0:
            start = jnp.where(row == OFF + BROW, north[at + 5 : at + 6, :], start)
        x = start + ((u_all[0, p] + u_all[1, p]) + (u_all[2, p] + u_all[3, p]))
        f_all[p] = x
        for q in range(BCOL):
            cols = slice(BX * q, BX * q + BX)
            natural[q, pl.ds(p, BROW, stride=BY), :] = x[OFF : OFF + BROW, cols]
            natural[BCOL + q, pl.ds(p, BROW, stride=BY), :] = r[OFF : OFF + BROW, cols]
    copies = []
    for k, out in enumerate((solution, residual)):
        for q in range(BCOL):
            n = BCOL * k + q
            copies.append(pltpu.make_async_copy(natural.at[n], out.at[:, pl.ds(BX * q, BX)], sems.at[n]))
    for copy in copies:
        copy.start()
    for p in range(BY):
        x = f_all[p]
        ocean = d_all[p] > 1.0
        above = f_all[p + 1] if p + 1 < BY else pltpu.roll(f_all[0], EXT - 1, 0)
        zonal = jnp.where(ocean, pltpu.roll(x, WIDE - 1, 1) - x, 0.0)
        meridional = jnp.where(ocean, above - x, 0.0)
        for q in range(BCOL):
            cols = slice(BX * q, BX * q + BX)
            g_all[q, EXT * p : EXT * p + EXT, :] = zonal[:, cols]
            g_all[BCOL + q, EXT * p : EXT * p + EXT, :] = meridional[:, cols]

    def take(slot, carry):
        index = loc[slot]
        row, col = (index >> 2) + OFF, index & 3
        slots[slot, 0] = g_all[col, pl.ds(row, BY, stride=EXT), :]
        slots[slot, 1] = g_all[BCOL + col, pl.ds(row, BY, stride=EXT), :]
        return carry

    lax.fori_loop(0, slots.shape[0], take, 0, unroll=8)
    for copy in copies:
        copy.wait()


def pick_kernel(dst, slots, out, sems):
    copies = [
        pltpu.make_async_copy(slots.at[dst[n]], out.at[n], sems.at[n]) for n in range(out.shape[0])
    ]
    for copy in copies:
        copy.start()
    for copy in copies:
        copy.wait()


def body(tendencies, thickness, ocean_blocks, land_mask, implicit_term, first_guess):
    nx = lax.axis_size("gx")
    ny = lax.axis_size("gy")
    gx = lax.axis_index("gx")
    gy = lax.axis_index("gy")
    devices = nx * ny
    listed = tendencies.shape[0]
    me = gx * ny + gy
    block_cols = BCOL * nx
    block_row = ocean_blocks // block_cols
    block_col = ocean_blocks % block_cols
    owner = block_col // BCOL * ny + block_row // BROW
    local = block_row % BROW * BCOL + block_col % BCOL
    dst = lax.dynamic_slice_in_dim(owner, me * listed, listed)
    loc = jnp.min(jnp.where(owner == me, local, BROW * BCOL).reshape(devices, listed), axis=1)
    device = jnp.arange(devices, dtype=jnp.int32)
    came = [(loc[None, :] == jnp.arange(BROW * BCOL, dtype=jnp.int32)[:, None])]
    for step, at in ((1, 0), (nx - 1, BCOL - 1)):
        here = (owner == (gx + step) % nx * ny + gy) & (local % BCOL == at)
        side = jnp.min(jnp.where(here, local // BCOL, BROW).reshape(devices, listed), axis=1)
        came.append(side[None, :] == jnp.arange(BROW, dtype=jnp.int32)[:, None])
    came = jnp.max(jnp.where(jnp.concatenate(came), device[None, :], 0), axis=1)
    flags = jnp.stack([gy % 2, (gy == ny - 1).astype(jnp.int32)]).astype(jnp.int32)

    east = [(i, (i + 1) % nx) for i in range(nx)]
    west = [(j, i) for i, j in east]
    swap_a, swap_b = [], []
    for i in range(nx):
        for j in range(ny):
            swap_a.append((i * ny + j, i * ny + (j ^ 1)))
            if j == ny - 1:
                swap_b.append((i * ny + j, (nx - 1 - i) * ny + j))
            elif j > 0:
                swap_b.append((i * ny + j, i * ny + (j + 1 if j % 2 else j - 1)))

    def exchange_x(to_east, to_west):
        return lax.ppermute(to_west, "gx", west), lax.ppermute(to_east, "gx", east)

    hbm = pl.BlockSpec(memory_space=pltpu.HBM)
    back = (devices, 2, BY, BX)
    sums = pl.pallas_call(
        sums_kernel,
        out_shape=jax.ShapeDtypeStruct((devices, 2 * BY // 4 + 1, 4, BX), F32),
        in_specs=[pl.BlockSpec(memory_space=pltpu.SMEM), hbm, hbm],
        out_specs=hbm,
        scratch_shapes=[
            pltpu.VMEM(tendencies.shape, tendencies.dtype),
            pltpu.SMEM(ocean_blocks.shape, jnp.int32),
            pltpu.VMEM((listed, 2 * BY // 4, 4, BX), F32),
            pltpu.VMEM((devices + 1, 4, BX), F32),
            pltpu.VMEM((LEV, BY, BX), F32),
            pltpu.SemaphoreType.DMA((listed // CHUNK,)),
            pltpu.SemaphoreType.DMA((listed,)),
            pltpu.SemaphoreType.DMA((2,)),
        ],
        compiler_params=pltpu.CompilerParams(vmem_limit_bytes=58 * MIB),
    )(thickness, ocean_blocks, tendencies)
    arrived = lax.all_to_all(sums, ("gx", "gy"), split_axis=0, concat_axis=0, tiled=True)

    own = (BY, EXT, BCOL * BX)
    tile = (BROW * BY, BCOL * BX)
    full = (BY, EXT, WIDE)
    strip = (STRIP, WIDE)
    sent = (SENT, BCOL * BX)
    sums, land_mask, implicit_term, first_guess = lax.optimization_barrier(
        (sums, land_mask, implicit_term, first_guess)
    )
    fields, to_east, to_west = call(
        prepare_kernel,
        [(2, *own), (2 * EXT, BX), (2 * EXT, BX)],
        [land_mask, implicit_term, first_guess],
        [(2 * BCOL, BROW * BY, BX)],
        58,
    )
    from_sides = exchange_x(to_east, to_west)

    small = (BY, 16, WIDE)
    first, second = call(
        ends_kernel,
        [sent, sent],
        [flags, came, arrived, fields, *from_sides],
        [(2 * (BCOL + 2), BY * 16, BX), small, small, small, small, small, small, strip, strip, strip],
        12,
    )
    came, first, second = lax.optimization_barrier((came, first, second))
    first = lax.ppermute(first, ("gx", "gy"), swap_a)
    second = lax.ppermute(second, ("gx", "gy"), swap_b)
    r_wide, d_wide, x_wide, inverse, edges = call(
        right_kernel,
        [full, full, full, full, (8, WIDE)],
        [came, arrived, fields, *from_sides],
        [(2 * (BCOL + 2), BY * EXT, BX), full],
        12,
    )
    vmem = pl.BlockSpec(memory_space=pltpu.VMEM)
    smem = pl.BlockSpec(memory_space=pltpu.SMEM)
    solution, residual, slots = pl.pallas_call(
        solve_kernel,
        out_shape=[jax.ShapeDtypeStruct(a, F32) for a in (tile, tile, back)],
        in_specs=[smem, smem] + [vmem] * 7,
        out_specs=[hbm, hbm, vmem],
        scratch_shapes=[pltpu.VMEM(full, F32)] * 5
        + [
            pltpu.VMEM((ITERS, *full), F32),
            pltpu.VMEM((2 * BCOL, BY * EXT, BX), F32),
            pltpu.VMEM((2 * BCOL, BROW * BY, BX), F32),
            pltpu.VMEM(strip, F32),
            pltpu.VMEM(strip, F32),
            pltpu.SemaphoreType.DMA((2 * BCOL,)),
        ],
        compiler_params=pltpu.CompilerParams(vmem_limit_bytes=18 * MIB),
    )(flags, loc, r_wide, d_wide, x_wide, inverse, edges, first, second)
    returned = lax.all_to_all(slots, ("gx", "gy"), split_axis=0, concat_axis=0, tiled=True)
    gradient_blocks = pl.pallas_call(
        pick_kernel,
        out_shape=jax.ShapeDtypeStruct((listed, 2, BY, BX), F32),
        in_specs=[pl.BlockSpec(memory_space=pltpu.SMEM), pl.BlockSpec(memory_space=pltpu.VMEM)],
        out_specs=pl.BlockSpec(memory_space=pl.ANY),
        scratch_shapes=[pltpu.SemaphoreType.DMA((listed,))],
        compiler_params=pltpu.CompilerParams(vmem_limit_bytes=4 * MIB),
    )(dst, returned)
    return solution, residual, gradient_blocks


def solution(mesh):
    placed = (
        P(("gx", "gy"), None, None, None, None),
        P(),
        P(),
        P("gy", "gx"),
        P("gy", "gx"),
        P("gy", "gx"),
    )
    return jax.shard_map(
        body,
        mesh=mesh,
        in_specs=placed,
        out_specs=(P("gy", "gx"), P("gy", "gx"), P(("gx", "gy"), None, None, None)),
        check_vma=False,
    )
```

time: 119 us -> 113 us (0.950)
  starting transfers between devices: 31.3 us -> 26.2 us
  waiting for transfers between devices: 60.3 us -> 55.2 us
  Pallas kernels: 23.1 us -> 26.5 us
    all_to_all x1, waiting for transfers between devices: 27.2 us -> 4.58 us  [body(): lax.all_to_all(sums, ('gx', 'gy'), split_axis=0, concat_axis=0, tiled=True)]
    ppermute x1, waiting for transfers between devices: 1.56 us -> 21.4 us  [exchange_x(): lax.ppermute(to_west, 'gx', west)]
    pallas_call x1 -> x2, Pallas kernels: 7.03 us -> 13.5 us  [the longest x1 7.42 us: body(): pl.pallas_call(sums_kernel, out_shape=jax.ShapeDtypeStruct((devices, 2 *...]
    all_to_all x1, starting transfers between devices: 16.3 us -> 11.8 us  [body(): lax.all_to_all(slots, ('gx', 'gy'), split_axis=0, concat_axis=0, tiled=True)]
    pallas_call x4 -> x3, Pallas kernels: 14.1 us -> 10.9 us  [call(): pl.pallas_call(kernel, out_shape=[jax.ShapeDtypeStruct(s, F32) for s in o...]
    ppermute x2, waiting for transfers between devices: 2.99 us -> 0.01 us  [the longest x1 0.01 us: body(): first = lax.ppermute(first, ('gx', 'gy'), swap_a)]
    unnamed x10 -> x6, local copies, waits for them, and re-layouts: 1.36 us -> 2.76 us
  transfers between devices with their start and end apart: 6 -> 6, of which waited for: 4 -> 3; matrix products, arithmetic and copies ran while one was open for 1% -> 1% of each run, Pallas kernels for 1% -> 6%
where the time goes in v2:
time: 113 us
  waiting for transfers between devices  55.2 us (49%)
  Pallas kernels  26.5 us (23%)
  starting transfers between devices  26.2 us (23%)
  local copies, waits for them, and re-layouts  3.06 us (3%)
    all_to_all x1, waiting for transfers between devices, body(): lax.all_to_all(slots, ('gx', 'gy'), split_axis=0, concat_axis=0, tiled=True)  29.2 us
    ppermute x1, waiting for transfers between devices, exchange_x(): lax.ppermute(to_west, 'gx', west)  21.4 us
    all_to_all x1, starting transfers between devices, body(): lax.all_to_all(slots, ('gx', 'gy'), split_axis=0, concat_axis=0, tiled=True)  11.8 us
    all_to_all x1, starting transfers between devices, body(): lax.all_to_all(sums, ('gx', 'gy'), split_axis=0, concat_axis=0, tiled=True)  11.5 us
    pallas_call x3, Pallas kernels, call(): pl.pallas_call(kernel, out_shape=[jax.ShapeDtypeStruct(s, F32) for s in o...  10.9 us
    pallas_call x1, Pallas kernels, body(): pl.pallas_call(sums_kernel, out_shape=jax.ShapeDtypeStruct((devices, 2 *...  7.42 us
    pallas_call x1, Pallas kernels, body(): pl.pallas_call(solve_kernel, out_shape=[jax.ShapeDtypeStruct(a, F32) for...  6.12 us
    all_to_all x1, waiting for transfers between devices, body(): lax.all_to_all(sums, ('gx', 'gy'), split_axis=0, concat_axis=0, tiled=True)  4.58 us
  transfers between devices with their start and end apart: 6, of which 3 were waited for; matrix products, arithmetic and copies ran while one was open for 1% of the time, Pallas kernels for 6%

profile of v2, /device:TPU:1, one launch (start us, length us, event | category | flops | bytes accessed | tf_op | source)
XLA Modules:
  0.0 112.6 jit_solution(1392860566252495627)
XLA Ops:
  0.6 7.4 %shard_map.85 = f32[128,9,4,128]{3,2,1,0:T(4,128)} custom-call(f32[24]{0:T(128)} %thickness.1, s32[8192]{0:T(1024)} %blocks.1, bf16[64,2,24,16,128]{4,3,2,1,0:T(8,128)(2,1)} %tendencies.1), custom_call_target="tpu_custom_call" | custom-call | tf_op jit(solution)/shard_map/pallas_call | solution.py:538
  8.1 11.5 %all-to-all-start = ((f32[128,9,4,128]{3,2,1,0:T(4,128)}), f32[128,9,4,128]{3,2,1,0:T(4,128)S(1)}, u32[]{:S(2)}, u32[]{:S(2)}) async-start(f32[128,9,4,128]{3,2,1,0:T(4,128)} %shard_map.85), calls=%async_computation | async-start | bytes 4718592 | tf_op jit(solution)/shard_map/all_to_all | solution.py:555
  19.6 3.4 %shard_map.86 = (f32[2,16,24,512]{3,2,1,0:T(8,128)}, f32[48,128]{1,0:T(8,128)}, f32[48,128]{1,0:T(8,128)}) custom-call(s32[320,512]{1,0:T(8,128)} %mask, f32[320,512]{1,0:T(8,128)} %implicit, f32[320,512]{1,0:T(8,128)} %guess), custom_call_target="tpu_custom_call" | custom-call | flops 1 | bytes 1 | tf_op jit(solution)/shard_map/pallas_call | solution.py:44
  23.0 1.1 collective-permute-start
  24.0 0.7 collective-permute-start.1
  24.7 0.1 and_select_fusion.1
  25.0 0.1 reduce_min.28
  25.1 0.1 reduce_min.29
  25.3 0.1 reduce_min.27.loc
  25.5 0.1 pad_add_fusion.flags
  25.6 0.1 select_reduce_fusion.came
  25.7 21.4 %collective-permute-done.east = f32[48,128]{1,0:T(8,128)S(1)} collective-permute-done((f32[48,128]{1,0:T(8,128)}, f32[48,128]{1,0:T(8,128)S(1)}, u32[]{:S(2)}, u32[]{:S(2)}) %collective-permute-start) | collective-permute-done | bytes 24608 | tf_op jit(solution)/shard_map/ppermute | solution.py:534
  47.1 4.6 %all-to-all-done.arrived = f32[128,9,4,128]{3,2,1,0:T(4,128)S(1)} async-done(((f32[128,9,4,128]{3,2,1,0:T(4,128)}), f32[128,9,4,128]{3,2,1,0:T(4,128)S(1)}, u32[]{:S(2)}, u32[]{:S(2)}) %all-to-all-start) | async-done | bytes 2359328 | tf_op jit(solution)/shard_map/all_to_all | solution.py:555
  51.7 1.4 %copy-done = f32[2,16,24,512]{3,2,1,0:T(8,128)S(1)} copy-done((f32[2,16,24,512]{3,2,1,0:T(8,128)S(1)}, f32[2,16,24,512]{3,2,1,0:T(8,128)}, u32[]{:S(2)}) %copy-start) | copy-done | bytes 1572888
  53.1 4.5 %shard_map.87 = (f32[40,512]{1,0:T(8,128)S(1)}, f32[40,512]{1,0:T(8,128)S(1)}) custom-call(s32[2]{0:T(128)S(1)} %pad_add_fusion.flags, s32[120]{0:T(128)S(1)} %select_reduce_fusion.came, f32[128,9,4,128]{3,2,1,0:T(4,128)S(1)} %all-to-all-done.arrived, f32[2,16,24,512]{3,2,1,0:T(8,128)S(1)} %copy-done, f32[48,128]{1,0:T(8,128)S(1)} %collective-permute-done.east, ...), custom_call_target="tpu_custom_call" | custom-call | flops 1 | bytes 1 | tf_op jit(solution)/shard_map/pallas_call | solution.py:44
  57.6 0.5 collective-permute-start.2
  58.1 0.7 collective-permute-start.3
  58.8 3.0 %shard_map.88 = (f32[16,24,640]{2,1,0:T(8,128)S(1)}, f32[16,24,640]{2,1,0:T(8,128)S(1)}, f32[16,24,640]{2,1,0:T(8,128)S(1)}, f32[16,24,640]{2,1,0:T(8,128)S(1)}, f32[8,640]{1,0:T(8,128)S(1)}) custom-call(s32[120]{0:T(128)S(1)} %select_reduce_fusion.came, f32[128,9,4,128]{3,2,1,0:T(4,128)S(1)} %all-to-all-done.arrived, f32[2,16,24,512]{3,2,1,0:T(8,128)S(1)} %copy-done, ...), custom_call_target="tpu_custom_call" | custom-call | flops 1 | bytes 1 | tf_op jit(solution)/shard_map/pallas_call | solution.py:44
  61.8 6.1 %shard_map.89 = (f32[320,512]{1,0:T(8,128)}, f32[320,512]{1,0:T(8,128)}, f32[128,2,16,128]{3,2,1,0:T(8,128)S(1)}) custom-call(s32[2]{0:T(128)S(1)} %pad_add_fusion.flags, s32[128]{0:T(128)S(1)} %reduce_min.27.loc, f32[16,24,640]{2,1,0:T(8,128)S(1)} %get-tuple-element.31.r_wide, f32[16,24,640]{2,1,0:T(8,128)S(1)} %get-tuple-element.32.d_wide, ...), custom_call_target="tpu_custom_call" | custom-call | tf_op jit(solution)/shard_map/pallas_call | solution.py:594
  67.9 1.3 %copy-done.1 = f32[128,2,16,128]{3,2,1,0:T(8,128)} copy-done((f32[128,2,16,128]{3,2,1,0:T(8,128)}, f32[128,2,16,128]{3,2,1,0:T(8,128)S(1)}, u32[]{:S(2)}) %copy-start.1) | copy-done | bytes 2097176
  69.3 11.8 %all-to-all-start.1 = ((f32[128,2,16,128]{3,2,1,0:T(8,128)}), f32[128,2,16,128]{3,2,1,0:T(8,128)S(1)}, u32[]{:S(2)}, u32[]{:S(2)}) async-start(f32[128,2,16,128]{3,2,1,0:T(8,128)} %copy-done.1), calls=%async_computation.1 | async-start | bytes 4194304 | tf_op jit(solution)/shard_map/all_to_all | solution.py:610
  81.1 0.1 dynamic_slice.3.dst
  81.2 29.2 %all-to-all-done.1.slots = f32[128,2,16,128]{3,2,1,0:T(8,128)S(1)} async-done(((f32[128,2,16,128]{3,2,1,0:T(8,128)}), f32[128,2,16,128]{3,2,1,0:T(8,128)S(1)}, u32[]{:S(2)}, u32[]{:S(2)}) %all-to-all-start.1) | async-done | bytes 2097184 | tf_op jit(solution)/shard_map/all_to_all | solution.py:610
  110.4 2.1 %shard_map.90 = f32[64,2,16,128]{3,2,1,0:T(8,128)} custom-call(s32[64]{0:T(128)S(1)} %dynamic_slice.3.dst, f32[128,2,16,128]{3,2,1,0:T(8,128)S(1)} %all-to-all-done.1.slots), custom_call_target="tpu_custom_call" | custom-call | tf_op jit(solution)/shard_map/pallas_call | solution.py:611
  (13 shorter events, 0.3 us)
Async XLA Ops:
  8.1 16.6 %copy-start.2 = (s32[8192]{0:T(1024)S(1)}, s32[8192]{0:T(1024)}, u32[]{:S(2)}) copy-start(s32[8192]{0:T(1024)} %blocks.1) | copy-start | bytes 98308
  8.1 43.6 %all-to-all-start = ((f32[128,9,4,128]{3,2,1,0:T(4,128)}), f32[128,9,4,128]{3,2,1,0:T(4,128)S(1)}, u32[]{:S(2)}, u32[]{:S(2)}) async-start(f32[128,9,4,128]{3,2,1,0:T(4,128)} %shard_map.85), calls=%async_computation | async-start | bytes 4718592 | tf_op jit(solution)/shard_map/all_to_all | solution.py:555
  23.0 24.1 %collective-permute-start = (f32[48,128]{1,0:T(8,128)}, f32[48,128]{1,0:T(8,128)S(1)}, u32[]{:S(2)}, u32[]{:S(2)}) collective-permute-start(f32[48,128]{1,0:T(8,128)} %get-tuple-element.26), channel_id=1, source_target_pairs={{8,0},{16,8},{24,16},{32,24},{40,32},{48,40},{56,48},{64,56},{72,6... | collective-permute-start | bytes 73736 | tf_op jit(solution)/shard_map/ppermute | solution.py:534
  24.0 23.1 %collective-permute-start.1 = (f32[48,128]{1,0:T(8,128)}, f32[48,128]{1,0:T(8,128)S(1)}, u32[]{:S(2)}, u32[]{:S(2)}) collective-permute-start(f32[48,128]{1,0:T(8,128)} %get-tuple-element.27), channel_id=1, source_target_pairs={{0,8},{8,16},{16,24},{24,32},{32,40},{40,48},{48,56},{56,64},{64,7... | collective-permute-start | bytes 73736 | tf_op jit(solution)/shard_map/ppermute | solution.py:534
  51.7 1.4 %copy-start = (f32[2,16,24,512]{3,2,1,0:T(8,128)S(1)}, f32[2,16,24,512]{3,2,1,0:T(8,128)}, u32[]{:S(2)}) copy-start(f32[2,16,24,512]{3,2,1,0:T(8,128)} %get-tuple-element.25.fields) | copy-start | bytes 4718596
  57.6 4.2 %collective-permute-start.2 = (f32[40,512]{1,0:T(8,128)S(1)}, f32[40,512]{1,0:T(8,128)S(1)}, u32[]{:S(2)}, u32[]{:S(2)}) collective-permute-start(f32[40,512]{1,0:T(8,128)S(1)} %get-tuple-element.36), channel_id=1, source_target_pairs={{0,1},{1,0},{2,3},{3,2},{4,5},{5,4},{6,7},{7,6},{8,9},{9,8},{10,11... | collective-permute-start | bytes 245768 | tf_op jit(solution)/shard_map/ppermute | solution.py:583
  58.1 3.7 %collective-permute-start.3 = (f32[40,512]{1,0:T(8,128)S(1)}, f32[40,512]{1,0:T(8,128)S(1)}, u32[]{:S(2)}, u32[]{:S(2)}) collective-permute-start(f32[40,512]{1,0:T(8,128)S(1)} %get-tuple-element.37), channel_id=1, source_target_pairs={{1,2},{2,1},{3,4},{4,3},{5,6},{6,5},{7,127},{9,10},{10,9},{11,12},... | collective-permute-start | bytes 245768 | tf_op jit(solution)/shard_map/ppermute | solution.py:584
  67.9 1.4 %copy-start.1 = (f32[128,2,16,128]{3,2,1,0:T(8,128)}, f32[128,2,16,128]{3,2,1,0:T(8,128)S(1)}, u32[]{:S(2)}) copy-start(f32[128,2,16,128]{3,2,1,0:T(8,128)S(1)} %get-tuple-element.40) | copy-start | bytes 6291460
  69.3 41.1 %all-to-all-start.1 = ((f32[128,2,16,128]{3,2,1,0:T(8,128)}), f32[128,2,16,128]{3,2,1,0:T(8,128)S(1)}, u32[]{:S(2)}, u32[]{:S(2)}) async-start(f32[128,2,16,128]{3,2,1,0:T(8,128)} %copy-done.1), calls=%async_computation.1 | async-start | bytes 4194304 | tf_op jit(solution)/shard_map/all_to_all | solution.py:610

commit v3 on v2

--- a/solution.py
+++ b/solution.py
@@ -233,7 +233,7 @@
                 work[(BCOL + 2) * part + BCOL + side, at_rows, :] = value
         return carry
 
-    lax.fori_loop(0, count, put, 0, unroll=4)
+    lax.fori_loop(0, count, put, 0, unroll=min(count, 10))
 
 
 def right_side(work, fields, east, west, parts, r_wide, d_wide, x_wide, inverse, tall):
@@ -480,17 +480,20 @@
         slots[slot, 1] = g_all[BCOL + col, pl.ds(row, BY, stride=EXT), :]
         return carry
 
-    lax.fori_loop(0, slots.shape[0], take, 0, unroll=8)
+    lax.fori_loop(0, slots.shape[0], take, 0, unroll=16)
     for copy in copies:
         copy.wait()
 
 
-def pick_kernel(dst, slots, out, sems):
-    copies = [
-        pltpu.make_async_copy(slots.at[dst[n]], out.at[n], sems.at[n]) for n in range(out.shape[0])
-    ]
-    for copy in copies:
-        copy.start()
+def pick_kernel(dst, slots, out, picked, sems):
+    part = picked.shape[0] // sems.shape[0]
+    copies = []
+    for c in range(sems.shape[0]):
+        for n in range(part * c, part * c + part):
+            picked[n] = slots[dst[n]]
+        at = pl.ds(part * c, part)
+        copies.append(pltpu.make_async_copy(picked.at[at], out.at[at], sems.at[c]))
+        copies[-1].start()
     for copy in copies:
         copy.wait()
 
@@ -613,7 +616,7 @@
         out_shape=jax.ShapeDtypeStruct((listed, 2, BY, BX), F32),
         in_specs=[pl.BlockSpec(memory_space=pltpu.SMEM), pl.BlockSpec(memory_space=pltpu.VMEM)],
         out_specs=pl.BlockSpec(memory_space=pl.ANY),
-        scratch_shapes=[pltpu.SemaphoreType.DMA((listed,))],
+        scratch_shapes=[pltpu.VMEM((listed, 2, BY, BX), F32), pltpu.SemaphoreType.DMA((4,))],
         compiler_params=pltpu.CompilerParams(vmem_limit_bytes=4 * MIB),
     )(dst, returned)
     return solution, residual, gradient_blocks

time: 113 us -> 112 us (level)
  no operation moved by 1% of the time
where the time goes in v3:
time: 112 us
  waiting for transfers between devices  55.2 us (49%)
  starting transfers between devices  26.4 us (24%)
  Pallas kernels  25.4 us (23%)
  local copies, waits for them, and re-layouts  3.06 us (3%)
    all_to_all x1, waiting for transfers between devices, body(): lax.all_to_all(slots, ('gx', 'gy'), split_axis=0, concat_axis=0, tiled=True)  29.2 us
    ppermute x1, waiting for transfers between devices, exchange_x(): lax.ppermute(to_west, 'gx', west)  21.4 us
    all_to_all x1, starting transfers between devices, body(): lax.all_to_all(slots, ('gx', 'gy'), split_axis=0, concat_axis=0, tiled=True)  12 us
    all_to_all x1, starting transfers between devices, body(): lax.all_to_all(sums, ('gx', 'gy'), split_axis=0, concat_axis=0, tiled=True)  11.5 us
    pallas_call x3, Pallas kernels, call(): pl.pallas_call(kernel, out_shape=[jax.ShapeDtypeStruct(s, F32) for s in o...  10.3 us
    pallas_call x1, Pallas kernels, body(): pl.pallas_call(sums_kernel, out_shape=jax.ShapeDtypeStruct((devices, 2 *...  7.42 us
    pallas_call x1, Pallas kernels, body(): pl.pallas_call(solve_kernel, out_shape=[jax.ShapeDtypeStruct(a, F32) for...  6.12 us
    all_to_all x1, waiting for transfers between devices, body(): lax.all_to_all(sums, ('gx', 'gy'), split_axis=0, concat_axis=0, tiled=True)  4.58 us
  transfers between devices with their start and end apart: 6, of which 3 were waited for; matrix products, arithmetic and copies ran while one was open for 1% of the time, Pallas kernels for 6%

profile of v3, /device:TPU:1, one launch (start us, length us, event | category | flops | bytes accessed | tf_op | source)
XLA Modules:
  0.0 111.6 jit_solution(10421910019210184502)
XLA Ops:
  0.6 7.4 %shard_map.85 = f32[128,9,4,128]{3,2,1,0:T(4,128)} custom-call(f32[24]{0:T(128)} %thickness.1, s32[8192]{0:T(1024)} %blocks.1, bf16[64,2,24,16,128]{4,3,2,1,0:T(8,128)(2,1)} %tendencies.1), custom_call_target="tpu_custom_call" | custom-call | tf_op jit(solution)/shard_map/pallas_call | solution.py:541
  8.1 11.5 %all-to-all-start = ((f32[128,9,4,128]{3,2,1,0:T(4,128)}), f32[128,9,4,128]{3,2,1,0:T(4,128)S(1)}, u32[]{:S(2)}, u32[]{:S(2)}) async-start(f32[128,9,4,128]{3,2,1,0:T(4,128)} %shard_map.85), calls=%async_computation | async-start | bytes 4718592 | tf_op jit(solution)/shard_map/all_to_all | solution.py:558
  19.6 3.4 %shard_map.86 = (f32[2,16,24,512]{3,2,1,0:T(8,128)}, f32[48,128]{1,0:T(8,128)}, f32[48,128]{1,0:T(8,128)}) custom-call(s32[320,512]{1,0:T(8,128)} %mask, f32[320,512]{1,0:T(8,128)} %implicit, f32[320,512]{1,0:T(8,128)} %guess), custom_call_target="tpu_custom_call" | custom-call | flops 1 | bytes 1 | tf_op jit(solution)/shard_map/pallas_call | solution.py:44
  23.0 1.1 collective-permute-start
  24.0 0.7 collective-permute-start.1
  24.7 0.1 and_select_fusion.1
  25.0 0.1 reduce_min.28
  25.1 0.1 reduce_min.29
  25.3 0.1 reduce_min.27.loc
  25.5 0.1 pad_add_fusion.flags
  25.6 0.1 select_reduce_fusion.came
  25.7 21.4 %collective-permute-done.east = f32[48,128]{1,0:T(8,128)S(1)} collective-permute-done((f32[48,128]{1,0:T(8,128)}, f32[48,128]{1,0:T(8,128)S(1)}, u32[]{:S(2)}, u32[]{:S(2)}) %collective-permute-start) | collective-permute-done | bytes 24608 | tf_op jit(solution)/shard_map/ppermute | solution.py:537
  47.1 4.6 %all-to-all-done.arrived = f32[128,9,4,128]{3,2,1,0:T(4,128)S(1)} async-done(((f32[128,9,4,128]{3,2,1,0:T(4,128)}), f32[128,9,4,128]{3,2,1,0:T(4,128)S(1)}, u32[]{:S(2)}, u32[]{:S(2)}) %all-to-all-start) | async-done | bytes 2359328 | tf_op jit(solution)/shard_map/all_to_all | solution.py:558
  51.7 1.4 %copy-done = f32[2,16,24,512]{3,2,1,0:T(8,128)S(1)} copy-done((f32[2,16,24,512]{3,2,1,0:T(8,128)S(1)}, f32[2,16,24,512]{3,2,1,0:T(8,128)}, u32[]{:S(2)}) %copy-start) | copy-done | bytes 1572888
  53.1 4.1 %shard_map.87 = (f32[40,512]{1,0:T(8,128)S(1)}, f32[40,512]{1,0:T(8,128)S(1)}) custom-call(s32[2]{0:T(128)S(1)} %pad_add_fusion.flags, s32[120]{0:T(128)S(1)} %select_reduce_fusion.came, f32[128,9,4,128]{3,2,1,0:T(4,128)S(1)} %all-to-all-done.arrived, f32[2,16,24,512]{3,2,1,0:T(8,128)S(1)} %copy-done, f32[48,128]{1,0:T(8,128)S(1)} %collective-permute-done.east, ...), custom_call_target="tpu_custom_call" | custom-call | flops 1 | bytes 1 | tf_op jit(solution)/shard_map/pallas_call | solution.py:44
  57.2 0.5 collective-permute-start.2
  57.6 0.7 collective-permute-start.3
  58.3 2.8 %shard_map.88 = (f32[16,24,640]{2,1,0:T(8,128)S(1)}, f32[16,24,640]{2,1,0:T(8,128)S(1)}, f32[16,24,640]{2,1,0:T(8,128)S(1)}, f32[16,24,640]{2,1,0:T(8,128)S(1)}, f32[8,640]{1,0:T(8,128)S(1)}) custom-call(s32[120]{0:T(128)S(1)} %select_reduce_fusion.came, f32[128,9,4,128]{3,2,1,0:T(4,128)S(1)} %all-to-all-done.arrived, f32[2,16,24,512]{3,2,1,0:T(8,128)S(1)} %copy-done, ...), custom_call_target="tpu_custom_call" | custom-call | flops 1 | bytes 1 | tf_op jit(solution)/shard_map/pallas_call | solution.py:44
  61.2 6.1 %shard_map.89 = (f32[320,512]{1,0:T(8,128)}, f32[320,512]{1,0:T(8,128)}, f32[128,2,16,128]{3,2,1,0:T(8,128)S(1)}) custom-call(s32[2]{0:T(128)S(1)} %pad_add_fusion.flags, s32[128]{0:T(128)S(1)} %reduce_min.27.loc, f32[16,24,640]{2,1,0:T(8,128)S(1)} %get-tuple-element.31.r_wide, f32[16,24,640]{2,1,0:T(8,128)S(1)} %get-tuple-element.32.d_wide, ...), custom_call_target="tpu_custom_call" | custom-call | tf_op jit(solution)/shard_map/pallas_call | solution.py:597
  67.3 1.3 %copy-done.1 = f32[128,2,16,128]{3,2,1,0:T(8,128)} copy-done((f32[128,2,16,128]{3,2,1,0:T(8,128)}, f32[128,2,16,128]{3,2,1,0:T(8,128)S(1)}, u32[]{:S(2)}) %copy-start.1) | copy-done | bytes 2097176
  68.7 12.0 %all-to-all-start.1 = ((f32[128,2,16,128]{3,2,1,0:T(8,128)}), f32[128,2,16,128]{3,2,1,0:T(8,128)S(1)}, u32[]{:S(2)}, u32[]{:S(2)}) async-start(f32[128,2,16,128]{3,2,1,0:T(8,128)} %copy-done.1), calls=%async_computation.1 | async-start | bytes 4194304 | tf_op jit(solution)/shard_map/all_to_all | solution.py:613
  80.6 0.1 dynamic_slice.3.dst
  80.7 29.2 %all-to-all-done.1.slots = f32[128,2,16,128]{3,2,1,0:T(8,128)S(1)} async-done(((f32[128,2,16,128]{3,2,1,0:T(8,128)}), f32[128,2,16,128]{3,2,1,0:T(8,128)S(1)}, u32[]{:S(2)}, u32[]{:S(2)}) %all-to-all-start.1) | async-done | bytes 2097184 | tf_op jit(solution)/shard_map/all_to_all | solution.py:613
  109.9 1.6 %shard_map.90 = f32[64,2,16,128]{3,2,1,0:T(8,128)} custom-call(s32[64]{0:T(128)S(1)} %dynamic_slice.3.dst, f32[128,2,16,128]{3,2,1,0:T(8,128)S(1)} %all-to-all-done.1.slots), custom_call_target="tpu_custom_call" | custom-call | tf_op jit(solution)/shard_map/pallas_call | solution.py:614
  (13 shorter events, 0.3 us)
Async XLA Ops:
  8.1 16.6 %copy-start.2 = (s32[8192]{0:T(1024)S(1)}, s32[8192]{0:T(1024)}, u32[]{:S(2)}) copy-start(s32[8192]{0:T(1024)} %blocks.1) | copy-start | bytes 98308
  8.1 43.6 %all-to-all-start = ((f32[128,9,4,128]{3,2,1,0:T(4,128)}), f32[128,9,4,128]{3,2,1,0:T(4,128)S(1)}, u32[]{:S(2)}, u32[]{:S(2)}) async-start(f32[128,9,4,128]{3,2,1,0:T(4,128)} %shard_map.85), calls=%async_computation | async-start | bytes 4718592 | tf_op jit(solution)/shard_map/all_to_all | solution.py:558
  23.0 24.1 %collective-permute-start = (f32[48,128]{1,0:T(8,128)}, f32[48,128]{1,0:T(8,128)S(1)}, u32[]{:S(2)}, u32[]{:S(2)}) collective-permute-start(f32[48,128]{1,0:T(8,128)} %get-tuple-element.26), channel_id=1, source_target_pairs={{8,0},{16,8},{24,16},{32,24},{40,32},{48,40},{56,48},{64,56},{72,6... | collective-permute-start | bytes 73736 | tf_op jit(solution)/shard_map/ppermute | solution.py:537
  24.0 23.1 %collective-permute-start.1 = (f32[48,128]{1,0:T(8,128)}, f32[48,128]{1,0:T(8,128)S(1)}, u32[]{:S(2)}, u32[]{:S(2)}) collective-permute-start(f32[48,128]{1,0:T(8,128)} %get-tuple-element.27), channel_id=1, source_target_pairs={{0,8},{8,16},{16,24},{24,32},{32,40},{40,48},{48,56},{56,64},{64,7... | collective-permute-start | bytes 73736 | tf_op jit(solution)/shard_map/ppermute | solution.py:537
  51.7 1.4 %copy-start = (f32[2,16,24,512]{3,2,1,0:T(8,128)S(1)}, f32[2,16,24,512]{3,2,1,0:T(8,128)}, u32[]{:S(2)}) copy-start(f32[2,16,24,512]{3,2,1,0:T(8,128)} %get-tuple-element.25.fields) | copy-start | bytes 4718596
  57.2 4.0 %collective-permute-start.2 = (f32[40,512]{1,0:T(8,128)S(1)}, f32[40,512]{1,0:T(8,128)S(1)}, u32[]{:S(2)}, u32[]{:S(2)}) collective-permute-start(f32[40,512]{1,0:T(8,128)S(1)} %get-tuple-element.36), channel_id=1, source_target_pairs={{0,1},{1,0},{2,3},{3,2},{4,5},{5,4},{6,7},{7,6},{8,9},{9,8},{10,11... | collective-permute-start | bytes 245768 | tf_op jit(solution)/shard_map/ppermute | solution.py:586
  57.6 3.5 %collective-permute-start.3 = (f32[40,512]{1,0:T(8,128)S(1)}, f32[40,512]{1,0:T(8,128)S(1)}, u32[]{:S(2)}, u32[]{:S(2)}) collective-permute-start(f32[40,512]{1,0:T(8,128)S(1)} %get-tuple-element.37), channel_id=1, source_target_pairs={{1,2},{2,1},{3,4},{4,3},{5,6},{6,5},{7,127},{9,10},{10,9},{11,12},... | collective-permute-start | bytes 245768 | tf_op jit(solution)/shard_map/ppermute | solution.py:587
  67.3 1.4 %copy-start.1 = (f32[128,2,16,128]{3,2,1,0:T(8,128)}, f32[128,2,16,128]{3,2,1,0:T(8,128)S(1)}, u32[]{:S(2)}) copy-start(f32[128,2,16,128]{3,2,1,0:T(8,128)S(1)} %get-tuple-element.40) | copy-start | bytes 6291460
  68.7 41.3 %all-to-all-start.1 = ((f32[128,2,16,128]{3,2,1,0:T(8,128)}), f32[128,2,16,128]{3,2,1,0:T(8,128)S(1)}, u32[]{:S(2)}, u32[]{:S(2)}) async-start(f32[128,2,16,128]{3,2,1,0:T(8,128)} %copy-done.1), calls=%async_computation.1 | async-start | bytes 4194304 | tf_op jit(solution)/shard_map/all_to_all | solution.py:613

commit v4 on v3

--- a/solution.py
+++ b/solution.py
@@ -569,7 +569,7 @@
         prepare_kernel,
         [(2, *own), (2 * EXT, BX), (2 * EXT, BX)],
         [land_mask, implicit_term, first_guess],
-        [(2 * BCOL, BROW * BY, BX)],
+        [(2 * BCOL + 1, BROW * BY, BX)],
         58,
     )
     from_sides = exchange_x(to_east, to_west)
@@ -603,7 +603,7 @@
         + [
             pltpu.VMEM((ITERS, *full), F32),
             pltpu.VMEM((2 * BCOL, BY * EXT, BX), F32),
-            pltpu.VMEM((2 * BCOL, BROW * BY, BX), F32),
+            pltpu.VMEM((2 * BCOL + 1, BROW * BY, BX), F32),
             pltpu.VMEM(strip, F32),
             pltpu.VMEM(strip, F32),
             pltpu.SemaphoreType.DMA((2 * BCOL,)),

time: 112 us -> 112 us (level)
  no operation moved by 1% of the time
where the time goes in v4:
time: 112 us
  waiting for transfers between devices  55.2 us (49%)
  starting transfers between devices  26.4 us (24%)
  Pallas kernels  25.4 us (23%)
  local copies, waits for them, and re-layouts  3.06 us (3%)
    all_to_all x1, waiting for transfers between devices, body(): lax.all_to_all(slots, ('gx', 'gy'), split_axis=0, concat_axis=0, tiled=True)  29.2 us
    ppermute x1, waiting for transfers between devices, exchange_x(): lax.ppermute(to_west, 'gx', west)  21.4 us
    all_to_all x1, starting transfers between devices, body(): lax.all_to_all(slots, ('gx', 'gy'), split_axis=0, concat_axis=0, tiled=True)  12 us
    all_to_all x1, starting transfers between devices, body(): lax.all_to_all(sums, ('gx', 'gy'), split_axis=0, concat_axis=0, tiled=True)  11.5 us
    pallas_call x3, Pallas kernels, call(): pl.pallas_call(kernel, out_shape=[jax.ShapeDtypeStruct(s, F32) for s in o...  10.3 us
    pallas_call x1, Pallas kernels, body(): pl.pallas_call(sums_kernel, out_shape=jax.ShapeDtypeStruct((devices, 2 *...  7.42 us
    pallas_call x1, Pallas kernels, body(): pl.pallas_call(solve_kernel, out_shape=[jax.ShapeDtypeStruct(a, F32) for...  6.12 us
    all_to_all x1, waiting for transfers between devices, body(): lax.all_to_all(sums, ('gx', 'gy'), split_axis=0, concat_axis=0, tiled=True)  4.58 us
  transfers between devices with their start and end apart: 6, of which 3 were waited for; matrix products, arithmetic and copies ran while one was open for 1% of the time, Pallas kernels for 6%

profile of v4, /device:TPU:1, one launch (start us, length us, event | category | flops | bytes accessed | tf_op | source)
XLA Modules:
  0.0 111.6 jit_solution(13353178755744370298)
XLA Ops:
  0.6 7.4 %shard_map.85 = f32[128,9,4,128]{3,2,1,0:T(4,128)} custom-call(f32[24]{0:T(128)} %thickness.1, s32[8192]{0:T(1024)} %blocks.1, bf16[64,2,24,16,128]{4,3,2,1,0:T(8,128)(2,1)} %tendencies.1), custom_call_target="tpu_custom_call" | custom-call | tf_op jit(solution)/shard_map/pallas_call | solution.py:541
  8.1 11.5 %all-to-all-start = ((f32[128,9,4,128]{3,2,1,0:T(4,128)}), f32[128,9,4,128]{3,2,1,0:T(4,128)S(1)}, u32[]{:S(2)}, u32[]{:S(2)}) async-start(f32[128,9,4,128]{3,2,1,0:T(4,128)} %shard_map.85), calls=%async_computation | async-start | bytes 4718592 | tf_op jit(solution)/shard_map/all_to_all | solution.py:558
  19.6 3.4 %shard_map.86 = (f32[2,16,24,512]{3,2,1,0:T(8,128)}, f32[48,128]{1,0:T(8,128)}, f32[48,128]{1,0:T(8,128)}) custom-call(s32[320,512]{1,0:T(8,128)} %mask, f32[320,512]{1,0:T(8,128)} %implicit, f32[320,512]{1,0:T(8,128)} %guess), custom_call_target="tpu_custom_call" | custom-call | flops 1 | bytes 1 | tf_op jit(solution)/shard_map/pallas_call | solution.py:44
  23.0 1.1 collective-permute-start
  24.0 0.7 collective-permute-start.1
  24.7 0.1 and_select_fusion.1
  25.0 0.1 reduce_min.28
  25.1 0.1 reduce_min.29
  25.3 0.1 reduce_min.27.loc
  25.5 0.1 pad_add_fusion.flags
  25.6 0.1 select_reduce_fusion.came
  25.7 21.4 %collective-permute-done.east = f32[48,128]{1,0:T(8,128)S(1)} collective-permute-done((f32[48,128]{1,0:T(8,128)}, f32[48,128]{1,0:T(8,128)S(1)}, u32[]{:S(2)}, u32[]{:S(2)}) %collective-permute-start) | collective-permute-done | bytes 24608 | tf_op jit(solution)/shard_map/ppermute | solution.py:537
  47.1 4.6 %all-to-all-done.arrived = f32[128,9,4,128]{3,2,1,0:T(4,128)S(1)} async-done(((f32[128,9,4,128]{3,2,1,0:T(4,128)}), f32[128,9,4,128]{3,2,1,0:T(4,128)S(1)}, u32[]{:S(2)}, u32[]{:S(2)}) %all-to-all-start) | async-done | bytes 2359328 | tf_op jit(solution)/shard_map/all_to_all | solution.py:558
  51.7 1.4 %copy-done = f32[2,16,24,512]{3,2,1,0:T(8,128)S(1)} copy-done((f32[2,16,24,512]{3,2,1,0:T(8,128)S(1)}, f32[2,16,24,512]{3,2,1,0:T(8,128)}, u32[]{:S(2)}) %copy-start) | copy-done | bytes 1572888
  53.1 4.1 %shard_map.87 = (f32[40,512]{1,0:T(8,128)S(1)}, f32[40,512]{1,0:T(8,128)S(1)}) custom-call(s32[2]{0:T(128)S(1)} %pad_add_fusion.flags, s32[120]{0:T(128)S(1)} %select_reduce_fusion.came, f32[128,9,4,128]{3,2,1,0:T(4,128)S(1)} %all-to-all-done.arrived, f32[2,16,24,512]{3,2,1,0:T(8,128)S(1)} %copy-done, f32[48,128]{1,0:T(8,128)S(1)} %collective-permute-done.east, ...), custom_call_target="tpu_custom_call" | custom-call | flops 1 | bytes 1 | tf_op jit(solution)/shard_map/pallas_call | solution.py:44
  57.1 0.5 collective-permute-start.2
  57.6 0.7 collective-permute-start.3
  58.3 2.8 %shard_map.88 = (f32[16,24,640]{2,1,0:T(8,128)S(1)}, f32[16,24,640]{2,1,0:T(8,128)S(1)}, f32[16,24,640]{2,1,0:T(8,128)S(1)}, f32[16,24,640]{2,1,0:T(8,128)S(1)}, f32[8,640]{1,0:T(8,128)S(1)}) custom-call(s32[120]{0:T(128)S(1)} %select_reduce_fusion.came, f32[128,9,4,128]{3,2,1,0:T(4,128)S(1)} %all-to-all-done.arrived, f32[2,16,24,512]{3,2,1,0:T(8,128)S(1)} %copy-done, ...), custom_call_target="tpu_custom_call" | custom-call | flops 1 | bytes 1 | tf_op jit(solution)/shard_map/pallas_call | solution.py:44
  61.2 6.1 %shard_map.89 = (f32[320,512]{1,0:T(8,128)}, f32[320,512]{1,0:T(8,128)}, f32[128,2,16,128]{3,2,1,0:T(8,128)S(1)}) custom-call(s32[2]{0:T(128)S(1)} %pad_add_fusion.flags, s32[128]{0:T(128)S(1)} %reduce_min.27.loc, f32[16,24,640]{2,1,0:T(8,128)S(1)} %get-tuple-element.31.r_wide, f32[16,24,640]{2,1,0:T(8,128)S(1)} %get-tuple-element.32.d_wide, ...), custom_call_target="tpu_custom_call" | custom-call | tf_op jit(solution)/shard_map/pallas_call | solution.py:597
  67.3 1.3 %copy-done.1 = f32[128,2,16,128]{3,2,1,0:T(8,128)} copy-done((f32[128,2,16,128]{3,2,1,0:T(8,128)}, f32[128,2,16,128]{3,2,1,0:T(8,128)S(1)}, u32[]{:S(2)}) %copy-start.1) | copy-done | bytes 2097176
  68.6 12.0 %all-to-all-start.1 = ((f32[128,2,16,128]{3,2,1,0:T(8,128)}), f32[128,2,16,128]{3,2,1,0:T(8,128)S(1)}, u32[]{:S(2)}, u32[]{:S(2)}) async-start(f32[128,2,16,128]{3,2,1,0:T(8,128)} %copy-done.1), calls=%async_computation.1 | async-start | bytes 4194304 | tf_op jit(solution)/shard_map/all_to_all | solution.py:613
  80.6 0.1 dynamic_slice.3.dst
  80.7 29.2 %all-to-all-done.1.slots = f32[128,2,16,128]{3,2,1,0:T(8,128)S(1)} async-done(((f32[128,2,16,128]{3,2,1,0:T(8,128)}), f32[128,2,16,128]{3,2,1,0:T(8,128)S(1)}, u32[]{:S(2)}, u32[]{:S(2)}) %all-to-all-start.1) | async-done | bytes 2097184 | tf_op jit(solution)/shard_map/all_to_all | solution.py:613
  109.9 1.6 %shard_map.90 = f32[64,2,16,128]{3,2,1,0:T(8,128)} custom-call(s32[64]{0:T(128)S(1)} %dynamic_slice.3.dst, f32[128,2,16,128]{3,2,1,0:T(8,128)S(1)} %all-to-all-done.1.slots), custom_call_target="tpu_custom_call" | custom-call | tf_op jit(solution)/shard_map/pallas_call | solution.py:614
  (13 shorter events, 0.3 us)
Async XLA Ops:
  8.1 16.6 %copy-start.2 = (s32[8192]{0:T(1024)S(1)}, s32[8192]{0:T(1024)}, u32[]{:S(2)}) copy-start(s32[8192]{0:T(1024)} %blocks.1) | copy-start | bytes 98308
  8.1 43.6 %all-to-all-start = ((f32[128,9,4,128]{3,2,1,0:T(4,128)}), f32[128,9,4,128]{3,2,1,0:T(4,128)S(1)}, u32[]{:S(2)}, u32[]{:S(2)}) async-start(f32[128,9,4,128]{3,2,1,0:T(4,128)} %shard_map.85), calls=%async_computation | async-start | bytes 4718592 | tf_op jit(solution)/shard_map/all_to_all | solution.py:558
  23.0 24.1 %collective-permute-start = (f32[48,128]{1,0:T(8,128)}, f32[48,128]{1,0:T(8,128)S(1)}, u32[]{:S(2)}, u32[]{:S(2)}) collective-permute-start(f32[48,128]{1,0:T(8,128)} %get-tuple-element.26), channel_id=1, source_target_pairs={{8,0},{16,8},{24,16},{32,24},{40,32},{48,40},{56,48},{64,56},{72,6... | collective-permute-start | bytes 73736 | tf_op jit(solution)/shard_map/ppermute | solution.py:537
  24.0 23.1 %collective-permute-start.1 = (f32[48,128]{1,0:T(8,128)}, f32[48,128]{1,0:T(8,128)S(1)}, u32[]{:S(2)}, u32[]{:S(2)}) collective-permute-start(f32[48,128]{1,0:T(8,128)} %get-tuple-element.27), channel_id=1, source_target_pairs={{0,8},{8,16},{16,24},{24,32},{32,40},{40,48},{48,56},{56,64},{64,7... | collective-permute-start | bytes 73736 | tf_op jit(solution)/shard_map/ppermute | solution.py:537
  51.7 1.4 %copy-start = (f32[2,16,24,512]{3,2,1,0:T(8,128)S(1)}, f32[2,16,24,512]{3,2,1,0:T(8,128)}, u32[]{:S(2)}) copy-start(f32[2,16,24,512]{3,2,1,0:T(8,128)} %get-tuple-element.25.fields) | copy-start | bytes 4718596
  57.1 4.0 %collective-permute-start.2 = (f32[40,512]{1,0:T(8,128)S(1)}, f32[40,512]{1,0:T(8,128)S(1)}, u32[]{:S(2)}, u32[]{:S(2)}) collective-permute-start(f32[40,512]{1,0:T(8,128)S(1)} %get-tuple-element.36), channel_id=1, source_target_pairs={{0,1},{1,0},{2,3},{3,2},{4,5},{5,4},{6,7},{7,6},{8,9},{9,8},{10,11... | collective-permute-start | bytes 245768 | tf_op jit(solution)/shard_map/ppermute | solution.py:586
  57.6 3.5 %collective-permute-start.3 = (f32[40,512]{1,0:T(8,128)S(1)}, f32[40,512]{1,0:T(8,128)S(1)}, u32[]{:S(2)}, u32[]{:S(2)}) collective-permute-start(f32[40,512]{1,0:T(8,128)S(1)} %get-tuple-element.37), channel_id=1, source_target_pairs={{1,2},{2,1},{3,4},{4,3},{5,6},{6,5},{7,127},{9,10},{10,9},{11,12},... | collective-permute-start | bytes 245768 | tf_op jit(solution)/shard_map/ppermute | solution.py:587
  67.3 1.4 %copy-start.1 = (f32[128,2,16,128]{3,2,1,0:T(8,128)}, f32[128,2,16,128]{3,2,1,0:T(8,128)S(1)}, u32[]{:S(2)}) copy-start(f32[128,2,16,128]{3,2,1,0:T(8,128)S(1)} %get-tuple-element.40) | copy-start | bytes 6291460
  68.6 41.3 %all-to-all-start.1 = ((f32[128,2,16,128]{3,2,1,0:T(8,128)}), f32[128,2,16,128]{3,2,1,0:T(8,128)S(1)}, u32[]{:S(2)}, u32[]{:S(2)}) async-start(f32[128,2,16,128]{3,2,1,0:T(8,128)} %copy-done.1), calls=%async_computation.1 | async-start | bytes 4194304 | tf_op jit(solution)/shard_map/all_to_all | solution.py:613
